TPU v7x, 128 devices: a whole 4x4x4 slice. The times are simulated.
128 devices in a mesh: row: 16 (over z_lo, x, core), col: 8 (over y, z_hi).
Axes of the slice: x: 4, y: 4, z: 4 (z_hi: 2, z_lo: 2; z = z_hi * 2 + z_lo), core: 2. Of those that a mesh axis runs over, the one named last changes fastest.
Arguments:
- front: float32 [12288, 12288], P('row', 'col'), as said below
- children: float32 [16384, 8192], P('row', 'col'), as said below
- maps: int32 [2, 64], replicated, may hold values from 0 to 95, as said below
Outputs:
- factored: float32 [12288, 12288], P('row', 'col')
Inputs may be any that keep to these rules, and one draw needn't show every extreme that they name: `maps`: each row increases, starts at 0 and ends at 95; each aligned run of 8 entries holds consecutive integers. Symmetric in matrix order; the assembled front is positive definite. `children`: each child's update is symmetric.
All inputs are finite; a program needn't handle non-finite values.
Results may differ from a plain program's by a relative error of at most 0.0003.
Values sent between devices are 32-bit elements; how exact they have to be, the bound alone decides.
A program may use at most 128 MiB of HBM per device.

v0:
```python
import jax
import jax.numpy as jnp
from jax import lax
from jax.sharding import PartitionSpec as P

BLOCK = 128
PANEL = 768
PANELS = 2


def from_root(value, axis, source):
    kept = jnp.where(lax.axis_index(axis) == source, value, 0).astype(value.dtype)
    return lax.psum(kept, axis)


def slot_position(blocks, owner_count):
    holder = blocks % owner_count
    length = blocks.shape[-1]
    shared = holder[..., :, None] == holder[..., None, :]
    before = jnp.arange(length)[None, :] < jnp.arange(length)[:, None]
    return (holder, jnp.sum(shared & before, axis=-1))


def pack_matrix(blocks, owner_count, capacity):
    holder, position = slot_position(blocks, owner_count)
    slot_ids = holder * capacity + position
    return (jnp.arange(owner_count * capacity)[:, None] == slot_ids[None, :]).astype(jnp.float32)


def place_matrix(blocks, self_index, owner_count, capacity, local_count, allowed):
    holder, position = slot_position(blocks, owner_count)
    sources = blocks.shape[0]
    column_ids = jnp.arange(sources)[:, None] * capacity + position
    usable = (holder == self_index) & allowed[:, None]
    local_index = blocks // owner_count
    targets = ((jnp.arange(local_count)[:, None, None] == local_index[None]) & usable[None]).astype(
        jnp.float32
    )
    columns = (jnp.arange(sources * capacity)[:, None, None] == column_ids[None]).astype(
        jnp.float32
    )
    return jnp.einsum("lsg,csg->lc", targets, columns)


def shards(front, children, maps):
    precise = lax.Precision.HIGHEST
    panel_blocks = PANEL // BLOCK
    row_count = lax.axis_size("row")
    col_count = lax.axis_size("col")
    row_self = lax.axis_index("row")
    col_self = lax.axis_index("col")
    run_length = children.shape[1] // BLOCK
    row_blocks = front.shape[0] // BLOCK
    col_blocks = front.shape[1] // BLOCK
    row_slots = (run_length + row_count - 1) // row_count
    col_slots = (run_length + col_count - 1) // col_count
    block_runs = maps.reshape(2, col_count, run_length)
    flat_runs = maps.reshape(2 * col_count, run_length)
    my_rows = lax.dynamic_index_in_dim(flat_runs, row_self, 0, keepdims=False)
    every_column = jnp.ones((col_count,), bool)
    owner_child = jnp.arange(row_count) // col_count
    width = children.shape[1]
    pack_rows = pack_matrix(my_rows, row_count, row_slots)
    held_rows = children.reshape(run_length, BLOCK * width)
    outgoing = jnp.dot(pack_rows, held_rows, precision=precise).reshape(
        row_count * row_slots * BLOCK, width
    )
    arrived = lax.all_to_all(outgoing, "row", split_axis=0, concat_axis=0, tiled=True).reshape(
        row_count * row_slots, BLOCK * width
    )
    place_rows = jnp.stack(
        [
            place_matrix(
                flat_runs, row_self, row_count, row_slots, row_blocks, owner_child == member
            )
            for member in range(2)
        ]
    )
    placed = jnp.einsum("kls,sx->klx", place_rows, arrived, precision=precise).reshape(
        2, row_blocks * BLOCK, run_length, BLOCK
    )
    my_columns = lax.dynamic_index_in_dim(block_runs, col_self, 1, keepdims=False)
    pack_columns = jnp.stack(
        [pack_matrix(my_columns[member], col_count, col_slots) for member in range(2)]
    )
    outgoing = jnp.einsum("kcg,krgb->krcb", pack_columns, placed, precision=precise).reshape(
        2, row_blocks * BLOCK, col_count * col_slots * BLOCK
    )
    arrived = lax.all_to_all(outgoing, "col", split_axis=2, concat_axis=2, tiled=True).reshape(
        2, row_blocks * BLOCK, col_count * col_slots, BLOCK
    )
    place_columns = jnp.stack(
        [
            place_matrix(
                block_runs[member], col_self, col_count, col_slots, col_blocks, every_column
            )
            for member in range(2)
        ]
    )
    added = jnp.einsum("klc,krcb->rlb", place_columns, arrived, precision=precise).reshape(
        row_blocks * BLOCK, col_blocks * BLOCK
    )
    matrix = front + added
    row_local = jnp.arange(row_blocks * BLOCK)
    col_local = jnp.arange(col_blocks * BLOCK)
    row_global = (row_local // BLOCK * row_count + row_self) * BLOCK + row_local % BLOCK
    col_global = (col_local // BLOCK * col_count + col_self) * BLOCK + col_local % BLOCK
    steps_in = jnp.arange(PANEL)
    ratio = row_count // col_count
    for panel_index in range(PANELS):
        start_col = panel_index * PANEL
        start_blk = panel_index * panel_blocks
        pieces = []
        for i in range(panel_blocks):
            block_id = start_blk + i
            local_index = block_id // col_count
            owned = (col_self == block_id % col_count).astype(jnp.float32)
            pieces.append(matrix[:, local_index * BLOCK : (local_index + 1) * BLOCK] * owned)
        panel_rows = lax.psum(jnp.concatenate(pieces, 1), "col")
        pieces = []
        for i in range(panel_blocks):
            block_id = start_blk + i
            local_index = block_id // row_count
            owned = (row_self == block_id % row_count).astype(jnp.float32)
            pieces.append(panel_rows[local_index * BLOCK : (local_index + 1) * BLOCK] * owned)
        pivot = lax.psum(jnp.concatenate(pieces, 0), "row")
        factor = jnp.linalg.cholesky(pivot)
        solved = jax.scipy.linalg.solve_triangular(factor, panel_rows.T, lower=True).T
        lower_part = jnp.where(row_global[:, None] >= start_col + steps_in[None, :], solved, 0.0)
        trailing = jnp.where(row_global[:, None] >= start_col + PANEL, solved, 0.0)
        for i in range(panel_blocks):
            block_id = start_blk + i
            local_index = block_id // col_count
            current = matrix[:, local_index * BLOCK : (local_index + 1) * BLOCK]
            chosen = jnp.where(
                col_self == block_id % col_count,
                lower_part[:, i * BLOCK : (i + 1) * BLOCK],
                current,
            )
            matrix = matrix.at[:, local_index * BLOCK : (local_index + 1) * BLOCK].set(chosen)
        copies = [from_root(trailing, "row", col_self + t * col_count) for t in range(ratio)]
        mirrored = (
            jnp.stack(copies)
            .reshape(ratio, row_blocks, BLOCK, PANEL)
            .transpose(1, 0, 2, 3)
            .reshape(col_blocks * BLOCK, PANEL)
        )
        matrix = matrix - lax.dot_general(
            trailing, mirrored, (((1,), (1,)), ((), ())), precision=precise
        )
    boundary = PANELS * PANEL
    return jnp.where(
        (row_global[:, None] < boundary) & (col_global[None, :] >= boundary), 0.0, matrix
    )


def solution(mesh):
    in_specs = (P("row", "col"), P("row", "col"), P())
    out_specs = P("row", "col")
    return jax.shard_map(shards, mesh=mesh, in_specs=in_specs, out_specs=out_specs, check_vma=False)
```

profile of v0, /device:TPU:39, one launch (start us, length us, event | category | flops | bytes accessed | tf_op | source)
XLA Modules:
  0.0 1619.0 jit_solution(7387739247984750795)
XLA Ops:
  7.5 4.9 reshape.1000
  12.5 7.0 fusion.168
  19.5 8.1 copy.95
  27.6 6.7 all-to-all-start
  35.2 108.7 %all-to-all-done = f32[16,128,1024]{2,1,0:T(8,128)} async-done(((f32[16,128,1024]{2,1,0:T(8,128)}), f32[16,128,1024]{2,1,0:T(8,128)}, u32[]{:S(2)}, u32[]{:S(2)}) %all-to-all-start) | async-done | bytes 8388640 | tf_op jit(solution)/shard_map/all_to_all | solution.py:68
  143.8 6.2 reshape.1038
  150.0 12.8 fusion.147
  162.8 7.2 reshape.1002
  170.0 8.4 convolution_bitcast_fusion
  178.4 7.7 copy.121
  186.0 6.6 all-to-all-start.1
  192.6 12.9 all-reduce.10.cloned.1.call-start
  206.6 6.0 copy.105
  213.1 66.5 %all-to-all-done.1 = f32[2,768,1024]{1,0,2:T(2,128)} async-done(((f32[2,768,1024]{1,0,2:T(2,128)}), f32[2,768,1024]{1,0,2:T(2,128)}, u32[]{:S(2)}, u32[]{:S(2)}) %all-to-all-start.1) | async-done | bytes 6291488 | tf_op jit(solution)/shard_map/all_to_all | solution.py:89
  279.6 7.9 copy.122
  287.5 9.2 convolution_bitcast_fusion.1
  296.7 6.4 copy.104
  303.1 4.4 bitcast_add_fusion
  311.2 119.7 %all-reduce.10.cloned.1.call-done = f32[768,768]{0,1:T(8,128)} async-done(((f32[768,768]{0,1:T(8,128)}), f32[768,768]{0,1:T(8,128)}) %all-reduce.10.cloned.1.call-update) | async-done | bytes 2359312 | tf_op jit(solution)/shard_map/psum | solution.py:119
  435.8 126.9 %all-reduce.12.cloned.1.call-done = f32[768,768]{0,1:T(8,128)} async-done(((f32[768,768]{0,1:T(8,128)}), f32[768,768]{0,1:T(8,128)}) %all-reduce.12.cloned.1.call-update) | async-done | bytes 2359312 | tf_op jit(solution)/shard_map/psum | solution.py:126
  562.7 3.2 copy.106
  569.3 11.7 cholesky.453
  581.2 9.8 custom-call.41
  593.8 11.7 cholesky.472
  606.9 10.2 custom-call.42
  619.0 11.7 cholesky.493
  631.5 9.8 custom-call.43
  643.2 11.9 cholesky.512
  655.7 9.8 custom-call.44
  667.3 11.7 cholesky.531
  679.7 9.8 custom-call.45
  691.1 12.1 cholesky.548
  709.1 17.1 %while.16 = (s32[]{:T(128)}, f32[768,768]{1,0:T(8,128)}, s32[6,2]{0,1:T(2,128)S(1)}, f32[6,128,128]{2,1,0:T(8,128)S(1)}, s32[]{:T(128)}) while((s32[]{:T(128)}, f32[768,768]{1,0:T(8,128)}, s32[6,2]{0,1:T(2,128)S(1)}, f32[6,128,128]{2,1,0:T(8,128)S(1)}, s32[]{:T(128)}) %tuple.147), condition=%wide.while_cond.12, body=%wide.while_body.12.sunk | while | flops 2 | bytes 131181 | solution.py:128
  726.2 59.0 %custom-call.46 = f32[6,128,128]{1,2,0:T(8,128)S(1)} custom-call(f32[6,128,128]{2,1,0:T(8,128)S(1)} %get-tuple-element.165), custom_call_target="InvertDiagBlocksLowerTriangular" | custom-call | tf_op jit(solution)/shard_map/jit(_solve_triangular)/triangular_solve | solution.py:128
  798.4 2.9 fusion.3
  801.3 3.0 copy.107
  804.3 3.1 copy.108
  817.4 122.3 %all-reduce.20.cloned.1.call-done = (f32[1,6,128,768]{3,2,1,0:T(8,128)}, f32[1,6,128,768]{3,2,1,0:T(8,128)}) async-done(((f32[1,6,128,768]{3,2,1,0:T(8,128)}, f32[1,6,128,768]{3,2,1,0:T(8,128)}), (f32[1,6,128,768]{3,2,1,0:T(8,128)}, f32[1,6,128,768]{3,2,1,0:T(8,128)})) %all-reduce.20.cloned.1.call-update) | async-done | bytes 4718608 | tf_op jit(solution)/shard_map/psum | solution.py:13
  939.6 2.8 maximum_bitcast_fusion
  944.5 12.1 convolution_subtract_fusion
  960.3 116.4 %all-reduce.14.cloned.1.call-done = f32[768,768]{0,1:T(8,128)} async-done(((f32[768,768]{0,1:T(8,128)}), f32[768,768]{0,1:T(8,128)}) %all-reduce.14.cloned.1.call-update) | async-done | bytes 2359312 | tf_op jit(solution)/shard_map/psum | solution.py:119
  1081.6 127.0 %all-reduce.16.cloned.1.call-done = f32[768,768]{0,1:T(8,128)} async-done(((f32[768,768]{0,1:T(8,128)}), f32[768,768]{0,1:T(8,128)}) %all-reduce.16.cloned.1.call-update) | async-done | bytes 2359312 | tf_op jit(solution)/shard_map/psum | solution.py:126
  1208.5 3.2 copy.111
  1215.1 11.7 cholesky.563
  1227.0 9.8 custom-call.47
  1239.6 11.7 cholesky.582
  1252.7 9.9 custom-call.48
  1264.6 11.7 cholesky.603
  1277.1 9.8 custom-call.49
  1288.8 11.9 cholesky.622
  1301.4 9.8 custom-call.50
  1313.0 11.7 cholesky.641
  1325.4 9.8 custom-call.51
  1336.8 12.1 cholesky.658
  1355.1 17.4 %while.17 = (s32[]{:T(128)}, f32[768,768]{1,0:T(8,128)}, s32[6,2]{0,1:T(2,128)S(1)}, f32[6,128,128]{2,1,0:T(8,128)S(1)}, s32[]{:T(128)}) while((s32[]{:T(128)}, f32[768,768]{1,0:T(8,128)}, s32[6,2]{0,1:T(2,128)S(1)}, f32[6,128,128]{2,1,0:T(8,128)S(1)}, s32[]{:T(128)}) %tuple.167), condition=%wide.while_cond.12.clone, body=%wide.while_body.12.clone.sunk | while | flops 2 | bytes 131181 | solution.py:128
  1372.5 59.0 %custom-call.52 = f32[6,128,128]{1,2,0:T(8,128)S(1)} custom-call(f32[6,128,128]{2,1,0:T(8,128)S(1)} %get-tuple-element.166), custom_call_target="InvertDiagBlocksLowerTriangular" | custom-call | tf_op jit(solution)/shard_map/jit(_solve_triangular)/triangular_solve | solution.py:128
  1444.7 2.8 fusion.5
  1447.6 3.3 copy.112
  1450.8 3.1 copy.113
  1454.6 4.8 copy.207
  1470.7 115.5 %all-reduce.18.cloned.1.call-done = (f32[1,6,128,768]{3,2,1,0:T(8,128)}, f32[1,6,128,768]{3,2,1,0:T(8,128)}) async-done(((f32[1,6,128,768]{3,2,1,0:T(8,128)}, f32[1,6,128,768]{3,2,1,0:T(8,128)}), (f32[1,6,128,768]{3,2,1,0:T(8,128)}, f32[1,6,128,768]{3,2,1,0:T(8,128)})) %all-reduce.18.cloned.1.call-update) | async-done | bytes 4718608 | tf_op jit(solution)/shard_map/psum | solution.py:13
  1586.2 2.7 maximum_bitcast_fusion.1
  1590.5 15.4 subtract_select_fusion
  1605.9 6.0 copy.116
  (258 shorter events, 144.8 us)
Async XLA Ops:
  27.6 6.7 copy-start.18
  27.6 116.2 %all-to-all-start = ((f32[16,128,1024]{2,1,0:T(8,128)}), f32[16,128,1024]{2,1,0:T(8,128)}, u32[]{:S(2)}, u32[]{:S(2)}) async-start(f32[16,128,1024]{2,1,0:T(8,128)} %copy.95), calls=%async_computation | async-start | bytes 16777216 | tf_op jit(solution)/shard_map/all_to_all | solution.py:68
  186.0 93.5 %all-to-all-start.1 = ((f32[2,768,1024]{1,0,2:T(2,128)}), f32[2,768,1024]{1,0,2:T(2,128)}, u32[]{:S(2)}, u32[]{:S(2)}) async-start(f32[2,768,1024]{1,0,2:T(2,128)} %bitcast.245), calls=%async_computation.1 | async-start | bytes 12582912 | tf_op jit(solution)/shard_map/all_to_all | solution.py:89
  192.6 238.2 %all-reduce.10.cloned.1.call-start = ((), (), s32[]{:S(2)}) async-start(), calls=%async_computation.2 | async-start | bytes 4718592 | tf_op jit(solution)/shard_map/psum | solution.py:119
  307.5 2.2 copy-start
  309.7 1.4 copy-start.17
  311.1 251.6 %all-reduce.12.cloned.1.call-start = ((), (), s32[]{:S(2)}) async-start(), calls=%async_computation.3 | async-start | bytes 4718592 | tf_op jit(solution)/shard_map/psum | solution.py:126
  430.9 3.2 copy-start.8
  434.2 1.4 copy-start.14
  435.7 503.9 %all-reduce.20.cloned.1.call-start = ((), (), s32[]{:S(2)}) async-start(), calls=%async_computation.7 | async-start | bytes 9437184 | tf_op jit(solution)/shard_map/psum | solution.py:13
  562.7 3.2 copy-start.6
  567.9 1.4 copy-start.12
  726.2 62.5 %copy-start.9 = (f32[768,768]{0,1:T(8,128)S(1)}, f32[768,768]{0,1:T(8,128)}, u32[]{:S(2)}) copy-start(f32[768,768]{0,1:T(8,128)} %all-reduce.10.cloned.1.call-done) | copy-start | bytes 7077892
  798.4 2.9 copy-start.2
  807.5 269.2 %all-reduce.14.cloned.1.call-start = ((), (), s32[]{:S(2)}) async-start(), calls=%async_computation.4 | async-start | bytes 4718592 | tf_op jit(solution)/shard_map/psum | solution.py:119
  939.6 3.6 slice-start
  942.5 1.2 slice-start.1
  942.5 2.0 copy-start.3
  956.6 2.2 copy-start.1
  958.8 1.4 copy-start.15
  960.2 248.3 %all-reduce.16.cloned.1.call-start = ((), (), s32[]{:S(2)}) async-start(), calls=%async_computation.5 | async-start | bytes 4718592 | tf_op jit(solution)/shard_map/psum | solution.py:126
  1076.7 3.2 copy-start.10
  1080.0 1.4 copy-start.16
  1081.5 504.7 %all-reduce.18.cloned.1.call-start = ((), (), s32[]{:S(2)}) async-start(), calls=%async_computation.6 | async-start | bytes 9437184 | tf_op jit(solution)/shard_map/psum | solution.py:13
  1208.5 3.2 copy-start.7
  1213.7 1.4 copy-start.13
  1372.5 62.6 %copy-start.11 = (f32[768,768]{0,1:T(8,128)S(1)}, f32[768,768]{0,1:T(8,128)}, u32[]{:S(2)}) copy-start(f32[768,768]{0,1:T(8,128)} %all-reduce.14.cloned.1.call-done) | copy-start | bytes 7077892
  1444.7 2.8 copy-start.4
  1588.9 1.7 copy-start.5
Sparse Core Ops, SparseCore 0:
  311.2 119.5 all-reduce.9
  435.8 126.8 all-reduce.11
  807.6 132.0 all-reduce.19
  960.4 116.2 all-reduce.13
  1081.6 126.8 all-reduce.15
  1454.0 132.0 all-reduce.17
where the time goes:
time: 1630 us; the launch traced here: 1620 us
  waiting for transfers between devices  903 us (55%)
  other arithmetic  419 us (26%)
  local copies, waits for them, and re-layouts  136 us (8%)
  matrix products  112 us (7%)
  starting transfers between devices  26.4 us (2%)
  between operations  22.3 us (1%)
    psum x2, waiting for transfers between devices, shards(): pivot = lax.psum(jnp.concatenate(pieces, 0), 'row')  254 us
    another operation x46, other arithmetic, shards(): factor = jnp.linalg.cholesky(pivot)  249 us
    psum x2, waiting for transfers between devices, from_root(): return lax.psum(kept, axis)  238 us
    psum x2, waiting for transfers between devices, shards(): panel_rows = lax.psum(jnp.concatenate(pieces, 1), 'col')  236 us
    another operation x5, other arithmetic, shards(): jax.scipy.linalg.solve_triangular(factor, panel_rows.T, lower=True)  121 us
    all_to_all x1, waiting for transfers between devices, shards(): lax.all_to_all(outgoing, 'row', split_axis=0, concat_axis=0, tiled=True)  109 us
    all_to_all x1, waiting for transfers between devices, shards(): lax.all_to_all(outgoing, 'col', split_axis=2, concat_axis=2, tiled=True)  66.5 us
    another operation x39, local copies, waits for them, and re-layouts, shards(): jax.scipy.linalg.solve_triangular(factor, panel_rows.T, lower=True)  34.3 us
  transfers between devices with their start and end apart: 8, of which 8 were waited for; matrix products, arithmetic and copies ran while one was open for 2% of the time, Pallas kernels for 0%

commit v1 on v0

v1 whole, which is shorter than its diff:
```python
import jax
import jax.numpy as jnp
from jax import lax
from jax.experimental import pallas as pl
from jax.experimental.pallas import tpu as pltpu
from jax.sharding import PartitionSpec as P

HIGHEST = lax.Precision.HIGHEST
MESH = pl.DeviceIdType.MESH
F32 = jnp.float32
BF16 = jnp.bfloat16
NN = (((1,), (0,)), ((), ()))
NT = (((1,), (1,)), ((), ()))
VMEM = pl.BlockSpec(memory_space=pltpu.VMEM)
SMEM = pl.BlockSpec(memory_space=pltpu.SMEM)
VMEM_LIMIT = 60 * 2**20


def run_of(maps_ref, member, block):
    run = jnp.int32(0)
    found = jnp.int32(0)
    for j in range(8):
        start = maps_ref[member, 8 * j]
        hit = ((block >= start) & (block < start + 8)).astype(jnp.int32)
        run = jnp.maximum(run, hit * j)
        found = jnp.maximum(found, hit)
    return run, found


def extend_kernel(maps_ref, child_ref, front_ref, out_ref, blocks, packed, arrived, send_sem, recv_sem):
    row, col = lax.axis_index("row"), lax.axis_index("col")
    me = row * 8 + col

    def peer(o):
        return lax.rem(row + o // 8, 16), lax.rem(col + lax.rem(o, 8), 8)

    barrier = pltpu.get_barrier_semaphore()

    @pl.loop(1, 128)
    def _(o):
        pl.semaphore_signal(barrier, inc=1, device_id=peer(o), device_id_type=MESH)

    for g in range(8):
        for h in range(8):
            blocks[g * 8 + h] = child_ref[128 * g : 128 * g + 128, 128 * h : 128 * h + 128]
    member = row // 8
    row_start = maps_ref[member, 8 * lax.rem(row, 8)]
    col_start = maps_ref[member, 8 * col]

    @pl.loop(0, 64)
    def _(p):
        g = lax.rem(p // 8 - lax.rem(row_start, 8) + 8, 8)
        h = lax.rem(lax.rem(p, 8) - lax.rem(col_start, 8) + 8, 8)
        packed[p] = blocks[g * 8 + h]

    arrived[me] = packed[lax.rem(row, 8) * 8 + col]
    pl.semaphore_wait(barrier, 127)

    @pl.loop(1, 128)
    def _(o):
        to_row, to_col = peer(o)
        pltpu.make_async_remote_copy(
            src_ref=packed.at[lax.rem(to_row, 8) * 8 + to_col],
            dst_ref=arrived.at[me],
            send_sem=send_sem,
            recv_sem=recv_sem,
            device_id=(to_row, to_col),
            device_id_type=MESH,
        ).start()

    everything = pltpu.make_async_remote_copy(
        src_ref=arrived.at[pl.ds(0, 127)],
        dst_ref=arrived.at[pl.ds(0, 127)],
        send_sem=send_sem,
        recv_sem=recv_sem,
        device_id=peer(1),
        device_id_type=MESH,
    )
    everything.wait_recv()

    @pl.loop(0, 6)
    def _(l):
        runs = [run_of(maps_ref, k, l * 16 + row) for k in range(2)]
        rows = pl.ds(pl.multiple_of(l * 128, 128), 128)

        @pl.loop(0, 12)
        def _(m):
            cols = pl.ds(pl.multiple_of(m * 128, 128), 128)
            total = front_ref[rows, cols]
            for k in range(2):
                run, found = runs[k]
                other, also = run_of(maps_ref, k, m * 8 + col)
                update = arrived[(k * 8 + run) * 8 + other]
                total = total + update * (found * also).astype(F32)
            out_ref[rows, cols] = total

    everything.wait_send()


def extend(maps, children, front):
    return pl.pallas_call(
        extend_kernel,
        out_shape=jax.ShapeDtypeStruct(front.shape, F32),
        in_specs=[SMEM, VMEM, VMEM],
        out_specs=VMEM,
        scratch_shapes=[
            pltpu.VMEM((64, 128, 128), F32),
            pltpu.VMEM((64, 128, 128), F32),
            pltpu.VMEM((128, 128, 128), F32),
            pltpu.SemaphoreType.DMA,
            pltpu.SemaphoreType.DMA,
        ],
        compiler_params=pltpu.CompilerParams(
            collective_id=0, has_side_effects=True, vmem_limit_bytes=VMEM_LIMIT
        ),
        name="extend_add",
    )(maps, children, front)


class Mover:
    def __init__(self, send_sem):
        self.send_sem = send_sem
        self.sent = []

    def send(self, guard, src, dst, recv_sem, target):
        copy = pltpu.make_async_remote_copy(
            src_ref=src,
            dst_ref=dst,
            send_sem=self.send_sem.at[len(self.sent)],
            recv_sem=recv_sem,
            device_id=target,
            device_id_type=MESH,
        )
        self.sent.append((guard, copy))

        @pl.when(guard)
        def _():
            copy.start()

    def finish(self):
        for guard, copy in self.sent:

            @pl.when(guard)
            def _():
                copy.wait_send()


def await_copy(guard, dst, recv_sem, peer):
    @pl.when(guard)
    def _():
        pltpu.make_async_remote_copy(
            src_ref=dst,
            dst_ref=dst,
            send_sem=recv_sem,
            recv_sem=recv_sem,
            device_id=peer,
            device_id_type=MESH,
        ).wait_recv()


class RowGather:
    def __init__(self, mover, view, half, sem, needed, places):
        self.mover, self.view, self.half, self.sem, self.needed = mover, view, half, sem, needed
        (self.h, self.x, self.k), (self.z_peer, self.right, self.left, self.mate) = places

    def slot(self, h, x):
        return h * 8 + x * 2 + self.k

    def near(self, step):
        x = lax.rem(self.x + step + 4, 4)
        return [self.slot(self.h, x), self.slot(1 - self.h, x)]

    def whole(self, slot, target):
        v = self.view(slot)
        self.mover.send(self.needed(slot), v, v, self.sem.at[0, slot], target)

    def part(self, slot, i, target):
        v = self.half(slot, i)
        self.mover.send(self.needed(slot), v, v, self.sem.at[i, slot], target)

    def got(self, slot, peer):
        await_copy(self.needed(slot), self.view(slot), self.sem.at[0, slot], peer)

    def got_part(self, slot, i, peer):
        await_copy(self.needed(slot), self.half(slot, i), self.sem.at[i, slot], peer)

    def to_pair(self):
        own = self.slot(self.h, self.x)
        self.whole(own, self.z_peer)
        self.whole(own, self.right)
        self.whole(own, self.left)
        self.whole(own, self.mate)

    def to_ring(self):
        other = self.slot(1 - self.h, self.x)
        self.got(other, self.z_peer)
        self.whole(other, self.right)
        self.whole(other, self.left)
        self.whole(other, self.mate)

    def forward(self):
        for slot in self.near(-1):
            self.got(slot, self.left)
            self.part(slot, 0, self.right)
        for slot in self.near(1):
            self.got(slot, self.right)
            self.part(slot, 1, self.left)
        for slot in self.near(-1) + self.near(1):
            self.whole(slot, self.mate)

    def to_mate(self):
        for slot in self.near(2):
            self.got_part(slot, 0, self.left)
            self.got_part(slot, 1, self.right)
            self.whole(slot, self.mate)

    def finish(self):
        for h in range(2):
            for x in range(4):
                slot = h * 8 + x * 2 + 1 - self.k
                self.got(slot, self.mate)


class ColGather:
    def __init__(self, mover, view, half, sem, places):
        self.mover, self.view, self.half, self.sem = mover, view, half, sem
        (self.y, self.s), (self.z_peer, self.right, self.left) = places

    def slots(self, y, s):
        return [y * 2 + s, y * 2 + s + 8]

    def both(self, step):
        y = lax.rem(self.y + step + 4, 4)
        return self.slots(y, 0) + self.slots(y, 1)

    def whole(self, slot, target):
        v = self.view(slot)
        self.mover.send(slot < 12, v, v, self.sem.at[0, slot], target)

    def part(self, slot, i, target):
        v = self.half(slot, i)
        self.mover.send(slot < 12, v, v, self.sem.at[i, slot], target)

    def got(self, slot, peer):
        await_copy(slot < 12, self.view(slot), self.sem.at[0, slot], peer)

    def got_part(self, slot, i, peer):
        await_copy(slot < 12, self.half(slot, i), self.sem.at[i, slot], peer)

    def to_pair(self):
        for slot in self.slots(self.y, self.s):
            self.whole(slot, self.z_peer)
            self.whole(slot, self.right)
            self.whole(slot, self.left)

    def to_ring(self):
        for slot in self.slots(self.y, 1 - self.s):
            self.got(slot, self.z_peer)
            self.whole(slot, self.right)
            self.whole(slot, self.left)

    def forward(self):
        for slot in self.both(-1):
            self.got(slot, self.left)
            self.part(slot, 0, self.right)
        for slot in self.both(1):
            self.got(slot, self.right)
            self.part(slot, 1, self.left)

    def finish(self):
        for slot in self.both(2):
            self.got_part(slot, 0, self.left)
            self.got_part(slot, 1, self.right)


def gather_kernel(
    a_ref, g1, g2, pv, send_sem, g1_sem, g2_sem, pv_sem
):
    row, col = lax.axis_index("row"), lax.axis_index("col")
    h, x, k = row // 8, lax.rem(row, 8) // 2, lax.rem(row, 2)
    y, s = col // 2, lax.rem(col, 2)
    at_x = lambda p: h * 8 + lax.rem(p + 4, 4) * 2 + k
    at_y = lambda p: lax.rem(p + 4, 4) * 2 + s
    row_peers = [
        ((1 - h) * 8 + x * 2 + k, col),
        (at_x(x + 1), col),
        (at_x(x - 1), col),
        (h * 8 + x * 2 + 1 - k, col),
    ]
    col_peers = [(row, y * 2 + 1 - s), (row, at_y(y + 1)), (row, at_y(y - 1))]
    barrier = pltpu.get_barrier_semaphore()
    for p in row_peers + col_peers:
        pl.semaphore_signal(barrier, inc=1, device_id=p, device_id_type=MESH)

    g2[col] = a_ref[:, 0:128].T

    @pl.when(col < 4)
    def _():
        g2[col + 8] = a_ref[:, 128:256].T

    @pl.when(row < 12)
    def _():
        g1[row] = a_ref[0:128, :]

    pl.semaphore_wait(barrier, 7)

    mover = Mover(send_sem)
    row_places = ((h, x, k), row_peers)
    wide = pl.ds(128, 1408)
    rows1 = RowGather(
        mover,
        lambda q: g1.at[q, :, wide],
        lambda q, i: g1.at[q, pl.ds(64 * i, 64), wide],
        g1_sem,
        lambda q: q < 12,
        row_places,
    )
    cols2 = ColGather(
        mover,
        lambda e: g2.at[e],
        lambda e, i: g2.at[e, pl.ds(64 * i, 64), :],
        g2_sem,
        ((y, s), col_peers),
    )

    def block_col(q):
        return pl.ds(pl.multiple_of(q * 128, 128), 128)

    pivots = [
        RowGather(
            mover,
            lambda q, t=t: pv.at[pl.ds(512 * t, 512), block_col(q)],
            lambda q, i, t=t: pv.at[pl.ds(512 * t + 256 * i, 256), block_col(q)],
            pv_sem.at[t],
            lambda q, t=t: q < 4 * (t + 1),
            row_places,
        )
        for t in range(3)
    ]
    cols2.to_pair()
    cols2.to_ring()
    rows1.to_pair()
    cols2.forward()
    rows1.to_ring()
    cols2.finish()

    @pl.when(row < 12)
    def _():
        @pl.loop(0, 12)
        def _(e):
            pv[pl.ds(pl.multiple_of(e * 128, 128), 128), block_col(row)] = g2[e, :, 0:128]

    for p in pivots:
        p.to_pair()
    for p in pivots:
        p.to_ring()
    rows1.forward()
    for p in pivots:
        p.forward()
    rows1.to_mate()
    for p in pivots:
        p.to_mate()
    for p in pivots:
        p.finish()
    rows1.finish()
    mover.finish()


def gather(a):
    return pl.pallas_call(
        gather_kernel,
        out_shape=(
            jax.ShapeDtypeStruct((12, 128, 1536), F32),
            jax.ShapeDtypeStruct((12, 128, 768), F32),
            jax.ShapeDtypeStruct((1536, 1536), F32),
        ),
        in_specs=[VMEM],
        out_specs=[VMEM] * 3,
        scratch_shapes=[
            pltpu.SemaphoreType.DMA((128,)),
            pltpu.SemaphoreType.DMA((2, 16)),
            pltpu.SemaphoreType.DMA((2, 16)),
            pltpu.SemaphoreType.DMA((3, 2, 16)),
        ],
        compiler_params=pltpu.CompilerParams(
            collective_id=1, has_side_effects=True, vmem_limit_bytes=VMEM_LIMIT
        ),
        name="gather_panel",
    )(a)


def factor128(a):
    rows = lax.broadcasted_iota(jnp.int32, (8, 128), 0)
    lanes = lax.broadcasted_iota(jnp.int32, (8, 128), 1)
    strips = [a[8 * g : 8 * g + 8, :] for g in range(16)]
    units = [jnp.where(lanes == rows + 8 * g, 1.0, 0.0).astype(jnp.float32) for g in range(16)]
    uppers, inverses = [], []
    full = (8, 128)
    for g in range(16):
        s, t = strips[g], units[g]
        cols = [jnp.broadcast_to(s[:, 8 * g + m : 8 * g + m + 1], full) for m in range(8)]
        e = [[jnp.broadcast_to(cols[m][i : i + 1, :], full) if i >= m else None for m in range(8)] for i in range(8)]
        z = [jnp.broadcast_to(s[i : i + 1, :], full) for i in range(8)]
        y = [jnp.broadcast_to(t[i : i + 1, :], full) for i in range(8)]
        l = [[None] * 8 for _ in range(8)]
        r = []
        for k in range(8):
            d = e[k][k]
            r0 = pl.reciprocal(d, approx=True)
            rk = r0 * (2.0 - d * r0)
            r.append(rk)
            for i in range(k + 1, 8):
                l[i][k] = e[i][k] * rk
            for j in range(k + 1, 8):
                for i in range(j, 8):
                    e[i][j] = e[i][j] - l[i][k] * e[j][k]
            for i in range(k + 1, 8):
                z[i] = z[i] - l[i][k] * z[k]
                y[i] = y[i] - l[i][k] * y[k]
        u = jnp.zeros(full, jnp.float32)
        w = jnp.zeros(full, jnp.float32)
        for i in range(8):
            d = e[i][i]
            q = lax.rsqrt(d)
            q = q * (1.5 - 0.5 * d * q * q)
            u = jnp.where(rows == i, z[i] * q, u)
            w = jnp.where(rows == i, y[i] * q, w)
        uppers.append(jnp.where(lanes >= rows + 8 * g, u, 0.0))
        inverses.append(w)
        if g == 15:
            break
        v = [None] * 8
        x = [None] * 8
        for i in reversed(range(8)):
            vi, xi = z[i] * r[i], y[i] * r[i]
            for m in range(i + 1, 8):
                vi = vi - l[m][i] * v[m]
                xi = xi - l[m][i] * x[m]
            v[i], x[i] = vi, xi
        for h in range(g + 1, 16):
            sh = strips[h]
            acc = [sh[:, 8 * g + m : 8 * g + m + 1] for m in range(8)]
            acc = [jnp.broadcast_to(c, full) for c in acc]
            p = [acc[m] * v[m] for m in range(8)]
            o = [acc[m] * x[m] for m in range(8)]
            while len(p) > 1:
                p = [p[2 * i] + p[2 * i + 1] for i in range(len(p) // 2)]
                o = [o[2 * i] + o[2 * i + 1] for i in range(len(o) // 2)]
            strips[h] = sh - p[0]
            units[h] = units[h] - o[0]
    return jnp.concatenate(uppers, 0), jnp.concatenate(inverses, 0)


def dot(a, b, dims=NN):
    return lax.dot_general(a, b, dims, precision=HIGHEST, preferred_element_type=jnp.float32)


def chol_loop(pv, dinv, nsteps=6):
    @pl.loop(0, nsteps)
    def _(J):
        ca = pl.multiple_of(J * 256, 256)
        cb = pl.multiple_of(J * 256 + 128, 128)
        ua, ia = factor128(pv[pl.ds(ca, 128), pl.ds(ca, 128)])
        la = ua.T
        pv[pl.ds(ca, 128), pl.ds(ca, 128)] = la
        wb = dot(pv[pl.ds(cb, 128), pl.ds(ca, 128)], ia, NT)
        pv[pl.ds(cb, 128), pl.ds(ca, 128)] = wb
        ub, ib = factor128(pv[pl.ds(cb, 128), pl.ds(cb, 128)] - dot(wb, wb, NT))
        pv[pl.ds(cb, 128), pl.ds(cb, 128)] = ub.T
        off = -dot(ib, dot(wb, ia))
        dinv[J, 0:128, 0:128] = ia
        dinv[J, 0:128, 128:256] = jnp.zeros((128, 128), jnp.float32)
        dinv[J, 128:256, 0:128] = off
        dinv[J, 128:256, 128:256] = ib
        inv = dinv[J]
        @pl.loop(J + 1, nsteps)
        def _(R):
            ro = pl.multiple_of(R * 256, 256)
            pv[pl.ds(ro, 256), pl.ds(ca, 256)] = dot(pv[pl.ds(ro, 256), pl.ds(ca, 256)], inv, NT)
        @pl.loop(J + 1, nsteps)
        def _(I):
            io = pl.multiple_of(I * 256, 256)
            wi = pv[pl.ds(io, 256), pl.ds(ca, 256)]
            @pl.loop(I, nsteps)
            def _(R):
                ro = pl.multiple_of(R * 256, 256)
                pv[pl.ds(ro, 256), pl.ds(io, 256)] -= dot(pv[pl.ds(ro, 256), pl.ds(ca, 256)], wi, NT)


def factor_kernel(p_ref, l_ref, d_ref):
    l_ref[...] = p_ref[...]
    chol_loop(l_ref, d_ref)


def factor(pv):
    return pl.pallas_call(
        factor_kernel,
        out_shape=(
            jax.ShapeDtypeStruct((1536, 1536), F32),
            jax.ShapeDtypeStruct((6, 256, 256), F32),
        ),
        in_specs=[VMEM],
        out_specs=[VMEM] * 2,
        compiler_params=pltpu.CompilerParams(vmem_limit_bytes=VMEM_LIMIT),
        name="factor",
    )(pv)


def split(v):
    hi = v.astype(BF16)
    return hi, (v - hi.astype(F32)).astype(BF16)


def dot3(ah, al, bh, bl):
    a = jnp.concatenate([ah, ah, al], 1)
    b = jnp.concatenate([bh, bl, bh], 0)
    return lax.dot_general(a, b, NN, preferred_element_type=F32)


def finish_kernel(a_ref, g1, g2, l_ref, d_ref, out_ref, xh, xl, yh, yl):
    row, col = lax.axis_index("row"), lax.axis_index("col")
    for i in range(6):
        dh, dl = split(d_ref[i])
        lh, ll = split(l_ref[256 * i : 256 * i + 256, : 256 * i]) if i else (None, None)

        def solve(rhs, cols):
            if i:
                rhs = rhs - dot3(lh, ll, xh[: 256 * i, cols], xl[: 256 * i, cols])
            hi, lo = split(dot3(dh, dl, *split(rhs)))
            xh[256 * i : 256 * i + 256, cols] = hi
            xl[256 * i : 256 * i + 256, cols] = lo

        @pl.loop(0, 2)
        def _(n):
            cols = pl.ds(pl.multiple_of(n * 768, 256), 768)
            solve(g1[2 * i : 2 * i + 2, :, cols].reshape(256, 768), cols)

        solve(g2[2 * i : 2 * i + 2].reshape(256, 768), pl.ds(1536, 768))
    for l in range(6):
        lanes = slice(1536 + 128 * l, 1664 + 128 * l)
        yh[128 * l : 128 * l + 128, :] = xh[:, lanes].T
        yl[128 * l : 128 * l + 128, :] = xl[:, lanes].T

    @pl.loop(0, 6)
    def _(t):
        rows = pl.ds(pl.multiple_of(t // 2 * 256, 256), 256)
        cols = pl.ds(pl.multiple_of(lax.rem(t, 2) * 768, 256), 768)
        out_ref[rows, cols] = a_ref[rows, cols] - dot3(
            yh[rows, :], yl[rows, :], xh[:, cols], xl[:, cols]
        )

    @pl.when(row < 12)
    def _():
        out_ref[0:128, :] = jnp.zeros((128, 1536), F32)

    def panel(block, m):
        lanes = pl.ds(pl.multiple_of(block * 128, 128), 128)
        values = yh[:, lanes].astype(F32) + yl[:, lanes].astype(F32)
        i = lax.broadcasted_iota(jnp.int32, values.shape, 0)
        j = lax.broadcasted_iota(jnp.int32, values.shape, 1)
        matrix_row = (i // 128 * 16 + row) * 128 + lax.rem(i, 128)
        out_ref[:, 128 * m : 128 * m + 128] = jnp.where(
            matrix_row >= block * 128 + j, values, 0.0
        )

    panel(col, 0)

    @pl.when(col < 4)
    def _():
        panel(col + 8, 1)


def finish(a, g1, g2, lower, inverses):
    return pl.pallas_call(
        finish_kernel,
        out_shape=jax.ShapeDtypeStruct(a.shape, F32),
        in_specs=[VMEM] * 5,
        out_specs=VMEM,
        scratch_shapes=[
            pltpu.VMEM((1536, 2304), BF16),
            pltpu.VMEM((1536, 2304), BF16),
            pltpu.VMEM((768, 1536), BF16),
            pltpu.VMEM((768, 1536), BF16),
        ],
        compiler_params=pltpu.CompilerParams(vmem_limit_bytes=VMEM_LIMIT),
        name="finish",
    )(a, g1, g2, lower, inverses)


def shards(front, children, maps):
    matrix = extend(maps, children, front)
    g1, g2, pv = gather(matrix)
    lower, inverses = factor(pv)
    return finish(matrix, g1, g2, lower, inverses)


def solution(mesh):
    in_specs = (P("row", "col"), P("row", "col"), P())
    out_specs = P("row", "col")
    return jax.shard_map(shards, mesh=mesh, in_specs=in_specs, out_specs=out_specs, check_vma=False)
```

time: 1630 us -> 442 us (0.27)
  waiting for transfers between devices: 903 us -> 0 us
  Pallas kernels: 0 us -> 441 us
  other arithmetic: 419 us -> 0 us
  local copies, waits for them, and re-layouts: 136 us -> 0 us
  matrix products: 112 us -> 0 us
  starting transfers between devices: 26.4 us -> 0 us
  between operations: 22.3 us -> 0.02 us
    psum x6 -> x0, waiting for transfers between devices: 728 us -> none  [the longest x2 254 us: shards(): pivot = lax.psum(jnp.concatenate(pieces, 0), 'row')]
    pallas_call x0 -> x4, Pallas kernels: none -> 441 us  [the longest x1 145 us: gather(): pl.pallas_call(gather_kernel, out_shape=(jax.ShapeDtypeStruct((12, 128, 1...]
    another operation x53 -> x0, other arithmetic: 371 us -> none  [the longest x46 249 us: shards(): factor = jnp.linalg.cholesky(pivot)]
    all_to_all x2 -> x0, waiting for transfers between devices: 175 us -> none  [the longest x1 109 us: shards(): lax.all_to_all(outgoing, 'row', split_axis=0, concat_axis=0, tiled=True)]
    dot_general x10 -> x0, matrix products: 65.6 us -> none  [the longest x2 27.5 us: shards(): lax.dot_general(trailing, mirrored, (((1,), (1,)), ((), ())), precision=p...]
    another operation x42 -> x0, matrix products: 46 us -> none  [the longest x22 26.4 us: shards(): jax.scipy.linalg.solve_triangular(factor, panel_rows.T, lower=True)]
    reshape x8 -> x0, local copies, waits for them, and re-layouts: 34.8 us -> none  [the longest x1 7.91 us: shards(): lax.all_to_all(outgoing, 'col', split_axis=2, concat_axis=2, tiled=True)]
    another operation x51 -> x0, local copies, waits for them, and re-layouts: 34.6 us -> none  [the longest x39 34.3 us: shards(): jax.scipy.linalg.solve_triangular(factor, panel_rows.T, lower=True)]
  transfers between devices with their start and end apart: 8 -> 0, of which waited for: 8 -> 0; matrix products, arithmetic and copies ran while one was open for 2% -> 0% of each run, Pallas kernels for 0% -> 0%
where the time goes in v1:
time: 442 us; the launch traced here: 441 us
  Pallas kernels  441 us (100%)
    pallas_call x1, Pallas kernels, gather(): pl.pallas_call(gather_kernel, out_shape=(jax.ShapeDtypeStruct((12, 128, 1...  145 us
    pallas_call x1, Pallas kernels, extend(): pl.pallas_call(extend_kernel, out_shape=jax.ShapeDtypeStruct(front.shape,...  129 us
    pallas_call x1, Pallas kernels, factor(): pl.pallas_call(factor_kernel, out_shape=(jax.ShapeDtypeStruct((1536, 1536...  116 us
    pallas_call x1, Pallas kernels, finish(): pl.pallas_call(finish_kernel, out_shape=jax.ShapeDtypeStruct(a.shape, F32...  51.2 us

profile of v1, /device:TPU:39, one launch (start us, length us, event | category | flops | bytes accessed | tf_op | source)
XLA Modules:
  0.0 441.4 jit_solution(2123105125252049311)
XLA Ops:
  0.0 129.3 %extend_add.1.a_ref = f32[768,1536]{1,0:T(8,128)} custom-call(s32[2,64]{1,0:T(2,128)} %maps_ref.1, f32[1024,1024]{1,0:T(8,128)} %child_ref.1, f32[768,1536]{1,0:T(8,128)} %front_ref.1), custom_call_target="tpu_custom_call" | custom-call | tf_op jit(solution)/shard_map/extend_add/pallas_call | solution.py:101
  129.3 144.5 %gather_panel.1 = (f32[12,128,1536]{2,1,0:T(8,128)}, f32[12,128,768]{2,1,0:T(8,128)}, f32[1536,1536]{1,0:T(8,128)}) custom-call(f32[768,1536]{1,0:T(8,128)} %extend_add.1.a_ref), custom_call_target="tpu_custom_call" | custom-call | tf_op jit(solution)/shard_map/gather_panel/pallas_call | solution.py:370
  273.8 116.4 %factor.1 = (f32[1536,1536]{1,0:T(8,128)}, f32[6,256,256]{2,1,0:T(8,128)}) custom-call(f32[1536,1536]{1,0:T(8,128)} %get-tuple-element.12.p_ref), custom_call_target="tpu_custom_call" | custom-call | tf_op jit(solution)/shard_map/factor/pallas_call | solution.py:496
  390.2 51.2 %finish.1 = f32[768,1536]{1,0:T(8,128)} custom-call(f32[768,1536]{1,0:T(8,128)} %extend_add.1.a_ref, f32[12,128,1536]{2,1,0:T(8,128)} %get-tuple-element.10.g1, f32[12,128,768]{2,1,0:T(8,128)} %get-tuple-element.11.g2, f32[1536,1536]{1,0:T(8,128)} %get-tuple-element.13.l_ref, f32[6,256,256]{2,1,0:T(8,128)} %get-tuple-element.14.d_ref), custom_call_target="tpu_custom_call" | custom-call | tf_op jit(solution)/shard_map/finish/pallas_call | solution.py:574

commit v2 on v1

--- a/solution.py
+++ b/solution.py
@@ -31,8 +31,16 @@
     row, col = lax.axis_index("row"), lax.axis_index("col")
     me = row * 8 + col
 
+    x, k, y = lax.rem(row, 8) // 2, lax.rem(row, 2), col // 2
+    z = lax.rem(col, 2) * 2 + row // 8
+
     def peer(o):
-        return lax.rem(row + o // 8, 16), lax.rem(col + lax.rem(o, 8), 8)
+        o = lax.rem(o * 29, 128)
+        to_x = lax.rem(x + lax.rem(o, 4), 4)
+        to_y = lax.rem(y + lax.rem(o // 4, 4), 4)
+        to_z = lax.rem(z + lax.rem(o // 16, 4), 4)
+        to_k = lax.rem(k + o // 64, 2)
+        return lax.rem(to_z, 2) * 8 + to_x * 2 + to_k, to_y * 2 + to_z // 2
 
     barrier = pltpu.get_barrier_semaphore()
 
@@ -122,27 +130,25 @@
         self.send_sem = send_sem
         self.sent = []
 
-    def send(self, guard, src, dst, recv_sem, target):
-        copy = pltpu.make_async_remote_copy(
-            src_ref=src,
-            dst_ref=dst,
-            send_sem=self.send_sem.at[len(self.sent)],
-            recv_sem=recv_sem,
-            device_id=target,
-            device_id_type=MESH,
-        )
+    def send(self, guard, ref, recv_sem, target):
+        number = len(self.sent)
+
+        def copy():
+            return pltpu.make_async_remote_copy(
+                src_ref=ref(),
+                dst_ref=ref(),
+                send_sem=self.send_sem.at[number],
+                recv_sem=recv_sem(),
+                device_id=target,
+                device_id_type=MESH,
+            )
+
         self.sent.append((guard, copy))
-
-        @pl.when(guard)
-        def _():
-            copy.start()
+        pl.when(guard())(lambda: copy().start())
 
     def finish(self):
         for guard, copy in self.sent:
-
-            @pl.when(guard)
-            def _():
-                copy.wait_send()
+            pl.when(guard())(lambda copy=copy: copy().wait_send())
 
 
 def await_copy(guard, dst, recv_sem, peer):
@@ -158,25 +164,22 @@
         ).wait_recv()
 
 
-class RowGather:
-    def __init__(self, mover, view, half, sem, needed, places):
+class Gather:
+    def __init__(self, mover, view, half, sem, needed):
         self.mover, self.view, self.half, self.sem, self.needed = mover, view, half, sem, needed
-        (self.h, self.x, self.k), (self.z_peer, self.right, self.left, self.mate) = places
-
-    def slot(self, h, x):
-        return h * 8 + x * 2 + self.k
-
-    def near(self, step):
-        x = lax.rem(self.x + step + 4, 4)
-        return [self.slot(self.h, x), self.slot(1 - self.h, x)]
 
     def whole(self, slot, target):
-        v = self.view(slot)
-        self.mover.send(self.needed(slot), v, v, self.sem.at[0, slot], target)
+        self.mover.send(
+            lambda: self.needed(slot), lambda: self.view(slot), lambda: self.sem.at[0, slot], target
+        )
 
     def part(self, slot, i, target):
-        v = self.half(slot, i)
-        self.mover.send(self.needed(slot), v, v, self.sem.at[i, slot], target)
+        self.mover.send(
+            lambda: self.needed(slot),
+            lambda: self.half(slot, i),
+            lambda: self.sem.at[i, slot],
+            target,
+        )
 
     def got(self, slot, peer):
         await_copy(self.needed(slot), self.view(slot), self.sem.at[0, slot], peer)
@@ -184,209 +187,75 @@
     def got_part(self, slot, i, peer):
         await_copy(self.needed(slot), self.half(slot, i), self.sem.at[i, slot], peer)
 
-    def to_pair(self):
-        own = self.slot(self.h, self.x)
-        self.whole(own, self.z_peer)
-        self.whole(own, self.right)
-        self.whole(own, self.left)
-        self.whole(own, self.mate)
-
-    def to_ring(self):
-        other = self.slot(1 - self.h, self.x)
-        self.got(other, self.z_peer)
-        self.whole(other, self.right)
-        self.whole(other, self.left)
-        self.whole(other, self.mate)
-
     def forward(self):
-        for slot in self.near(-1):
+        for slot in self.near[-1]:
             self.got(slot, self.left)
             self.part(slot, 0, self.right)
-        for slot in self.near(1):
+        for slot in self.near[1]:
             self.got(slot, self.right)
             self.part(slot, 1, self.left)
-        for slot in self.near(-1) + self.near(1):
+
+
+class RowGather(Gather):
+    def __init__(self, mover, view, half, sem, needed, places):
+        super().__init__(mover, view, half, sem, needed)
+        (h, x, k), (self.z_peer, self.right, self.left, self.mate) = places
+        at = lambda h, x, k: h * 8 + lax.rem(x + 4, 4) * 2 + k
+        self.own, self.other = at(h, x, k), at(1 - h, x, k)
+        self.near = {d: [at(h, x + d, k), at(1 - h, x + d, k)] for d in (-1, 1, 2)}
+        self.theirs = [at(g, jnp.int32(p), 1 - k) for g in range(2) for p in range(4)]
+
+    def to_pair(self):
+        for target in (self.z_peer, self.right, self.left, self.mate):
+            self.whole(self.own, target)
+
+    def to_ring(self):
+        self.got(self.other, self.z_peer)
+        for target in (self.right, self.left, self.mate):
+            self.whole(self.other, target)
+
+    def forward(self):
+        super().forward()
+        for slot in self.near[-1] + self.near[1]:
             self.whole(slot, self.mate)
 
     def to_mate(self):
-        for slot in self.near(2):
+        for slot in self.near[2]:
             self.got_part(slot, 0, self.left)
             self.got_part(slot, 1, self.right)
             self.whole(slot, self.mate)
 
     def finish(self):
-        for h in range(2):
-            for x in range(4):
-                slot = h * 8 + x * 2 + 1 - self.k
-                self.got(slot, self.mate)
-
-
-class ColGather:
+        for slot in self.theirs:
+            self.got(slot, self.mate)
+
+
+class ColGather(Gather):
     def __init__(self, mover, view, half, sem, places):
-        self.mover, self.view, self.half, self.sem = mover, view, half, sem
-        (self.y, self.s), (self.z_peer, self.right, self.left) = places
-
-    def slots(self, y, s):
-        return [y * 2 + s, y * 2 + s + 8]
-
-    def both(self, step):
-        y = lax.rem(self.y + step + 4, 4)
-        return self.slots(y, 0) + self.slots(y, 1)
-
-    def whole(self, slot, target):
-        v = self.view(slot)
-        self.mover.send(slot < 12, v, v, self.sem.at[0, slot], target)
-
-    def part(self, slot, i, target):
-        v = self.half(slot, i)
-        self.mover.send(slot < 12, v, v, self.sem.at[i, slot], target)
-
-    def got(self, slot, peer):
-        await_copy(slot < 12, self.view(slot), self.sem.at[0, slot], peer)
-
-    def got_part(self, slot, i, peer):
-        await_copy(slot < 12, self.half(slot, i), self.sem.at[i, slot], peer)
+        super().__init__(mover, view, half, sem, lambda e: e < 12)
+        (y, s), (self.z_peer, self.right, self.left) = places
+        at = lambda y, s: lax.rem(y + 4, 4) * 2 + s
+        self.own = [at(y, s), at(y, s) + 8]
+        self.other = [at(y, 1 - s), at(y, 1 - s) + 8]
+        self.near = {
+            d: [at(y + d, t) + e for t in range(2) for e in (0, 8)] for d in (-1, 1, 2)
+        }
 
     def to_pair(self):
-        for slot in self.slots(self.y, self.s):
-            self.whole(slot, self.z_peer)
-            self.whole(slot, self.right)
-            self.whole(slot, self.left)
+        for slot in self.own:
+            for target in (self.z_peer, self.right, self.left):
+                self.whole(slot, target)
 
     def to_ring(self):
-        for slot in self.slots(self.y, 1 - self.s):
+        for slot in self.other:
             self.got(slot, self.z_peer)
-            self.whole(slot, self.right)
-            self.whole(slot, self.left)
-
-    def forward(self):
-        for slot in self.both(-1):
-            self.got(slot, self.left)
-            self.part(slot, 0, self.right)
-        for slot in self.both(1):
-            self.got(slot, self.right)
-            self.part(slot, 1, self.left)
+            for target in (self.right, self.left):
+                self.whole(slot, target)
 
     def finish(self):
-        for slot in self.both(2):
+        for slot in self.near[2]:
             self.got_part(slot, 0, self.left)
             self.got_part(slot, 1, self.right)
-
-
-def gather_kernel(
-    a_ref, g1, g2, pv, send_sem, g1_sem, g2_sem, pv_sem
-):
-    row, col = lax.axis_index("row"), lax.axis_index("col")
-    h, x, k = row // 8, lax.rem(row, 8) // 2, lax.rem(row, 2)
-    y, s = col // 2, lax.rem(col, 2)
-    at_x = lambda p: h * 8 + lax.rem(p + 4, 4) * 2 + k
-    at_y = lambda p: lax.rem(p + 4, 4) * 2 + s
-    row_peers = [
-        ((1 - h) * 8 + x * 2 + k, col),
-        (at_x(x + 1), col),
-        (at_x(x - 1), col),
-        (h * 8 + x * 2 + 1 - k, col),
-    ]
-    col_peers = [(row, y * 2 + 1 - s), (row, at_y(y + 1)), (row, at_y(y - 1))]
-    barrier = pltpu.get_barrier_semaphore()
-    for p in row_peers + col_peers:
-        pl.semaphore_signal(barrier, inc=1, device_id=p, device_id_type=MESH)
-
-    g2[col] = a_ref[:, 0:128].T
-
-    @pl.when(col < 4)
-    def _():
-        g2[col + 8] = a_ref[:, 128:256].T
-
-    @pl.when(row < 12)
-    def _():
-        g1[row] = a_ref[0:128, :]
-
-    pl.semaphore_wait(barrier, 7)
-
-    mover = Mover(send_sem)
-    row_places = ((h, x, k), row_peers)
-    wide = pl.ds(128, 1408)
-    rows1 = RowGather(
-        mover,
-        lambda q: g1.at[q, :, wide],
-        lambda q, i: g1.at[q, pl.ds(64 * i, 64), wide],
-        g1_sem,
-        lambda q: q < 12,
-        row_places,
-    )
-    cols2 = ColGather(
-        mover,
-        lambda e: g2.at[e],
-        lambda e, i: g2.at[e, pl.ds(64 * i, 64), :],
-        g2_sem,
-        ((y, s), col_peers),
-    )
-
-    def block_col(q):
-        return pl.ds(pl.multiple_of(q * 128, 128), 128)
-
-    pivots = [
-        RowGather(
-            mover,
-            lambda q, t=t: pv.at[pl.ds(512 * t, 512), block_col(q)],
-            lambda q, i, t=t: pv.at[pl.ds(512 * t + 256 * i, 256), block_col(q)],
-            pv_sem.at[t],
-            lambda q, t=t: q < 4 * (t + 1),
-            row_places,
-        )
-        for t in range(3)
-    ]
-    cols2.to_pair()
-    cols2.to_ring()
-    rows1.to_pair()
-    cols2.forward()
-    rows1.to_ring()
-    cols2.finish()
-
-    @pl.when(row < 12)
-    def _():
-        @pl.loop(0, 12)
-        def _(e):
-            pv[pl.ds(pl.multiple_of(e * 128, 128), 128), block_col(row)] = g2[e, :, 0:128]
-
-    for p in pivots:
-        p.to_pair()
-    for p in pivots:
-        p.to_ring()
-    rows1.forward()
-    for p in pivots:
-        p.forward()
-    rows1.to_mate()
-    for p in pivots:
-        p.to_mate()
-    for p in pivots:
-        p.finish()
-    rows1.finish()
-    mover.finish()
-
-
-def gather(a):
-    return pl.pallas_call(
-        gather_kernel,
-        out_shape=(
-            jax.ShapeDtypeStruct((12, 128, 1536), F32),
-            jax.ShapeDtypeStruct((12, 128, 768), F32),
-            jax.ShapeDtypeStruct((1536, 1536), F32),
-        ),
-        in_specs=[VMEM],
-        out_specs=[VMEM] * 3,
-        scratch_shapes=[
-            pltpu.SemaphoreType.DMA((128,)),
-            pltpu.SemaphoreType.DMA((2, 16)),
-            pltpu.SemaphoreType.DMA((2, 16)),
-            pltpu.SemaphoreType.DMA((3, 2, 16)),
-        ],
-        compiler_params=pltpu.CompilerParams(
-            collective_id=1, has_side_effects=True, vmem_limit_bytes=VMEM_LIMIT
-        ),
-        name="gather_panel",
-    )(a)
 
 
 def factor128(a):
@@ -455,11 +324,13 @@
     return lax.dot_general(a, b, dims, precision=HIGHEST, preferred_element_type=jnp.float32)
 
 
-def chol_loop(pv, dinv, nsteps=6):
+def chol_loop(pv, dinv, between, nsteps=6):
     @pl.loop(0, nsteps)
     def _(J):
         ca = pl.multiple_of(J * 256, 256)
         cb = pl.multiple_of(J * 256 + 128, 128)
+        for step, action in enumerate(between):
+            pl.when(J == step)(action)
         ua, ia = factor128(pv[pl.ds(ca, 128), pl.ds(ca, 128)])
         la = ua.T
         pv[pl.ds(ca, 128), pl.ds(ca, 128)] = la
@@ -487,25 +358,6 @@
                 pv[pl.ds(ro, 256), pl.ds(io, 256)] -= dot(pv[pl.ds(ro, 256), pl.ds(ca, 256)], wi, NT)
 
 
-def factor_kernel(p_ref, l_ref, d_ref):
-    l_ref[...] = p_ref[...]
-    chol_loop(l_ref, d_ref)
-
-
-def factor(pv):
-    return pl.pallas_call(
-        factor_kernel,
-        out_shape=(
-            jax.ShapeDtypeStruct((1536, 1536), F32),
-            jax.ShapeDtypeStruct((6, 256, 256), F32),
-        ),
-        in_specs=[VMEM],
-        out_specs=[VMEM] * 2,
-        compiler_params=pltpu.CompilerParams(vmem_limit_bytes=VMEM_LIMIT),
-        name="factor",
-    )(pv)
-
-
 def split(v):
     hi = v.astype(BF16)
     return hi, (v - hi.astype(F32)).astype(BF16)
@@ -517,8 +369,7 @@
     return lax.dot_general(a, b, NN, preferred_element_type=F32)
 
 
-def finish_kernel(a_ref, g1, g2, l_ref, d_ref, out_ref, xh, xl, yh, yl):
-    row, col = lax.axis_index("row"), lax.axis_index("col")
+def finish_steps(row, col, a_ref, g1, g2, l_ref, d_ref, out_ref, xh, xl, yh, yl):
     for i in range(6):
         dh, dl = split(d_ref[i])
         lh, ll = split(l_ref[256 * i : 256 * i + 256, : 256 * i]) if i else (None, None)
@@ -553,7 +404,7 @@
     def _():
         out_ref[0:128, :] = jnp.zeros((128, 1536), F32)
 
-    def panel(block, m):
+    def place(block, m):
         lanes = pl.ds(pl.multiple_of(block * 128, 128), 128)
         values = yh[:, lanes].astype(F32) + yl[:, lanes].astype(F32)
         i = lax.broadcasted_iota(jnp.int32, values.shape, 0)
@@ -563,35 +414,149 @@
             matrix_row >= block * 128 + j, values, 0.0
         )
 
-    panel(col, 0)
+    place(col, 0)
 
     @pl.when(col < 4)
     def _():
-        panel(col + 8, 1)
-
-
-def finish(a, g1, g2, lower, inverses):
+        place(col + 8, 1)
+
+
+def panel_kernel(
+    a_ref, out_ref, g1, g2, pv, dinv, xh, xl, yh, yl, early_sem, send_sem, head_sem, g1_sem, g2_sem, pv_sem
+):
+    row, col = lax.axis_index("row"), lax.axis_index("col")
+    h, x, k = row // 8, lax.rem(row, 8) // 2, lax.rem(row, 2)
+    y, s = col // 2, lax.rem(col, 2)
+    at_x = lambda p: h * 8 + lax.rem(p + 4, 4) * 2 + k
+    at_y = lambda p: lax.rem(p + 4, 4) * 2 + s
+    row_peers = [
+        ((1 - h) * 8 + x * 2 + k, col),
+        (at_x(x + 1), col),
+        (at_x(x - 1), col),
+        (h * 8 + x * 2 + 1 - k, col),
+    ]
+    col_peers = [(row, y * 2 + 1 - s), (row, at_y(y + 1)), (row, at_y(y - 1))]
+    all_cols = [(row, lax.rem(col + o, 8)) for o in range(1, 8)]
+    barrier = pltpu.get_barrier_semaphore()
+    for p in row_peers + all_cols:
+        pl.semaphore_signal(barrier, inc=1, device_id=p, device_id_type=MESH)
+
+    g2[col] = a_ref[:, 0:128].T
+
+    @pl.when(col < 4)
+    def _():
+        g2[col + 8] = a_ref[:, 128:256].T
+
+    pl.semaphore_wait(barrier, 11)
+
+    early, mover = Mover(early_sem), Mover(send_sem)
+    row_places = ((h, x, k), row_peers)
+
+    def head(e):
+        return g2.at[e, :, pl.ds(0, 128)]
+
+    for p in all_cols:
+        early.send(lambda: col >= 0, lambda: head(col), lambda: head_sem.at[col], p)
+        early.send(lambda: col < 4, lambda: head(col + 8), lambda: head_sem.at[col + 8], p)
+
+    @pl.when(row < 12)
+    def _():
+        g1[row] = a_ref[0:128, :]
+
+    wide = pl.ds(128, 1408)
+    rows1 = RowGather(
+        mover,
+        lambda q: g1.at[q, :, wide],
+        lambda q, i: g1.at[q, pl.ds(64 * i, 64), wide],
+        g1_sem,
+        lambda q: q < 12,
+        row_places,
+    )
+    rest = pl.ds(128, 640)
+    cols2 = ColGather(
+        mover,
+        lambda e: g2.at[e, :, rest],
+        lambda e, i: g2.at[e, pl.ds(64 * i, 64), rest],
+        g2_sem,
+        ((y, s), col_peers),
+    )
+
+    def block_col(q):
+        return pl.ds(pl.multiple_of(q * 128, 128), 128)
+
+    pivots = [
+        RowGather(
+            early,
+            lambda q, t=t: pv.at[pl.ds(512 * t, 512), block_col(q)],
+            lambda q, i, t=t: pv.at[pl.ds(512 * t + 256 * i, 256), block_col(q)],
+            pv_sem.at[t],
+            lambda q, t=t: q < 4 * (t + 1),
+            row_places,
+        )
+        for t in range(3)
+    ]
+    for e in range(12):
+        await_copy(col != e % 8, head(e), head_sem.at[e], (row, e % 8))
+
+    @pl.when(row < 12)
+    def _():
+        @pl.loop(0, 12)
+        def _(e):
+            pv[pl.ds(pl.multiple_of(e * 128, 128), 128), block_col(row)] = g2[e, :, 0:128]
+
+    for p in pivots:
+        p.to_pair()
+    cols2.to_pair()
+    for p in pivots:
+        p.to_ring()
+    for p in pivots:
+        p.forward()
+    rows1.to_pair()
+    cols2.to_ring()
+    for p in pivots:
+        p.to_mate()
+    for p in pivots:
+        p.finish()
+    rows1.to_ring()
+    early.finish()
+    chol_loop(pv, dinv, [lambda: None, cols2.forward, rows1.forward, lambda: None, rows1.to_mate])
+    cols2.finish()
+    rows1.finish()
+    mover.finish()
+    finish_steps(row, col, a_ref, g1, g2, pv, dinv, out_ref, xh, xl, yh, yl)
+
+
+def panel(a):
     return pl.pallas_call(
-        finish_kernel,
+        panel_kernel,
         out_shape=jax.ShapeDtypeStruct(a.shape, F32),
-        in_specs=[VMEM] * 5,
+        in_specs=[VMEM],
         out_specs=VMEM,
         scratch_shapes=[
+            pltpu.VMEM((12, 128, 1536), F32),
+            pltpu.VMEM((12, 128, 768), F32),
+            pltpu.VMEM((1536, 1536), F32),
+            pltpu.VMEM((6, 256, 256), F32),
             pltpu.VMEM((1536, 2304), BF16),
             pltpu.VMEM((1536, 2304), BF16),
             pltpu.VMEM((768, 1536), BF16),
             pltpu.VMEM((768, 1536), BF16),
+            pltpu.SemaphoreType.DMA((96,)),
+            pltpu.SemaphoreType.DMA((64,)),
+            pltpu.SemaphoreType.DMA((16,)),
+            pltpu.SemaphoreType.DMA((2, 16)),
+            pltpu.SemaphoreType.DMA((2, 16)),
+            pltpu.SemaphoreType.DMA((3, 2, 16)),
         ],
-        compiler_params=pltpu.CompilerParams(vmem_limit_bytes=VMEM_LIMIT),
-        name="finish",
-    )(a, g1, g2, lower, inverses)
+        compiler_params=pltpu.CompilerParams(
+            collective_id=1, has_side_effects=True, vmem_limit_bytes=62 * 2**20
+        ),
+        name="panel",
+    )(a)
 
 
 def shards(front, children, maps):
-    matrix = extend(maps, children, front)
-    g1, g2, pv = gather(matrix)
-    lower, inverses = factor(pv)
-    return finish(matrix, g1, g2, lower, inverses)
+    return panel(extend(maps, children, front))
 
 
 def solution(mesh):

time: 442 us -> 365 us (0.83); the launches traced: 441 us -> 358 us
  Pallas kernels: 441 us -> 353 us
  local copies, waits for them, and re-layouts: 0 us -> 4.84 us
    pallas_call x3 -> x1, Pallas kernels: 312 us -> 222 us  [panel(): pl.pallas_call(panel_kernel, out_shape=jax.ShapeDtypeStruct(a.shape, F32)...]
    unnamed x0 -> x1, local copies, waits for them, and re-layouts: none -> 4.84 us
where the time goes in v2:
time: 365 us; the launch traced here: 358 us
  Pallas kernels  353 us (97%)
  local copies, waits for them, and re-layouts  4.84 us (1%)
    pallas_call x1, Pallas kernels, panel(): pl.pallas_call(panel_kernel, out_shape=jax.ShapeDtypeStruct(a.shape, F32)...  222 us
    pallas_call x1, Pallas kernels, extend(): pl.pallas_call(extend_kernel, out_shape=jax.ShapeDtypeStruct(front.shape,...  130 us

profile of v2, /device:TPU:39, one launch (start us, length us, event | category | flops | bytes accessed | tf_op | source)
XLA Modules:
  0.0 357.6 jit_solution(18368990519752730457)
XLA Ops:
  0.0 130.3 %extend_add.1.a_ref = f32[768,1536]{1,0:T(8,128)} custom-call(s32[2,64]{1,0:T(2,128)} %maps_ref.1, f32[1024,1024]{1,0:T(8,128)} %child_ref.1, f32[768,1536]{1,0:T(8,128)} %front_ref.1), custom_call_target="tpu_custom_call" | custom-call | tf_op jit(solution)/shard_map/extend_add/pallas_call | solution.py:109
  130.3 222.5 %panel.1 = f32[768,1536]{1,0:T(8,128)} custom-call(f32[768,1536]{1,0:T(8,128)} %extend_add.1.a_ref), custom_call_target="tpu_custom_call" | custom-call | tf_op jit(solution)/shard_map/panel/pallas_call | solution.py:530
  352.7 4.8 %copy.5 = f32[768,1536]{1,0:T(8,128)} copy(f32[768,1536]{1,0:T(8,128)} %panel.1) | data formatting | bytes 9437184

commit v3 on v2

v3 whole, which is shorter than its diff:
```python
import jax
import jax.numpy as jnp
from jax import lax
from jax.experimental import pallas as pl
from jax.experimental.pallas import tpu as pltpu
from jax.sharding import PartitionSpec as P

HIGHEST = lax.Precision.HIGHEST
MESH = pl.DeviceIdType.MESH
F32 = jnp.float32
BF16 = jnp.bfloat16
NN = (((1,), (0,)), ((), ()))
NT = (((1,), (1,)), ((), ()))
VMEM = pl.BlockSpec(memory_space=pltpu.VMEM)
SMEM = pl.BlockSpec(memory_space=pltpu.SMEM)
VMEM_LIMIT = 60 * 2**20


def run_of(maps_ref, member, block):
    run = jnp.int32(0)
    found = jnp.int32(0)
    for j in range(8):
        start = maps_ref[member, 8 * j]
        hit = ((block >= start) & (block < start + 8)).astype(jnp.int32)
        run = jnp.maximum(run, hit * j)
        found = jnp.maximum(found, hit)
    return run, found


class Mover:
    def __init__(self, send_sem):
        self.send_sem = send_sem
        self.sent = []

    def send(self, guard, ref, recv_sem, target, to=None):
        number = len(self.sent)

        def copy():
            return pltpu.make_async_remote_copy(
                src_ref=ref(),
                dst_ref=(to or ref)(),
                send_sem=self.send_sem.at[number],
                recv_sem=recv_sem(),
                device_id=target,
                device_id_type=MESH,
            )

        self.sent.append((guard, copy))
        pl.when(guard())(lambda: copy().start())

    def finish(self):
        for guard, copy in self.sent:
            pl.when(guard())(lambda copy=copy: copy().wait_send())


def await_copy(guard, dst, recv_sem, peer):
    @pl.when(guard)
    def _():
        pltpu.make_async_remote_copy(
            src_ref=dst,
            dst_ref=dst,
            send_sem=recv_sem,
            recv_sem=recv_sem,
            device_id=peer,
            device_id_type=MESH,
        ).wait_recv()


class Gather:
    def __init__(self, mover, view, half, sem, needed):
        self.mover, self.view, self.half, self.sem, self.needed = mover, view, half, sem, needed

    def whole(self, slot, target):
        self.mover.send(
            lambda: self.needed(slot), lambda: self.view(slot), lambda: self.sem.at[0, slot], target
        )

    def part(self, slot, i, target):
        self.mover.send(
            lambda: self.needed(slot),
            lambda: self.half(slot, i),
            lambda: self.sem.at[i, slot],
            target,
        )

    def got(self, slot, peer):
        await_copy(self.needed(slot), self.view(slot), self.sem.at[0, slot], peer)

    def got_part(self, slot, i, peer):
        await_copy(self.needed(slot), self.half(slot, i), self.sem.at[i, slot], peer)

    def forward(self):
        for slot in self.near[-1]:
            self.got(slot, self.left)
            self.part(slot, 0, self.right)
        for slot in self.near[1]:
            self.got(slot, self.right)
            self.part(slot, 1, self.left)


class RowGather(Gather):
    def __init__(self, mover, view, half, sem, needed, places):
        super().__init__(mover, view, half, sem, needed)
        (h, x, k), (self.z_peer, self.right, self.left, self.mate) = places
        at = lambda h, x, k: h * 8 + lax.rem(x + 4, 4) * 2 + k
        self.own, self.other = at(h, x, k), at(1 - h, x, k)
        self.near = {d: [at(h, x + d, k), at(1 - h, x + d, k)] for d in (-1, 1, 2)}
        self.theirs = [at(g, jnp.int32(p), 1 - k) for g in range(2) for p in range(4)]

    def to_pair(self):
        for target in (self.z_peer, self.right, self.left, self.mate):
            self.whole(self.own, target)

    def to_ring(self):
        self.got(self.other, self.z_peer)
        for target in (self.right, self.left, self.mate):
            self.whole(self.other, target)

    def forward(self):
        super().forward()
        for slot in self.near[-1] + self.near[1]:
            self.whole(slot, self.mate)

    def to_mate(self):
        for slot in self.near[2]:
            self.got_part(slot, 0, self.left)
            self.got_part(slot, 1, self.right)
            self.whole(slot, self.mate)

    def finish(self):
        for slot in self.theirs:
            self.got(slot, self.mate)


class ColGather(Gather):
    def __init__(self, mover, view, half, sem, places):
        super().__init__(mover, view, half, sem, lambda e: e < 12)
        (y, s), (self.z_peer, self.right, self.left) = places
        at = lambda y, s: lax.rem(y + 4, 4) * 2 + s
        self.own = [at(y, s), at(y, s) + 8]
        self.other = [at(y, 1 - s), at(y, 1 - s) + 8]
        self.near = {
            d: [at(y + d, t) + e for t in range(2) for e in (0, 8)] for d in (-1, 1, 2)
        }

    def to_pair(self):
        for slot in self.own:
            for target in (self.z_peer, self.right, self.left):
                self.whole(slot, target)

    def to_ring(self):
        for slot in self.other:
            self.got(slot, self.z_peer)
            for target in (self.right, self.left):
                self.whole(slot, target)

    def finish(self):
        for slot in self.near[2]:
            self.got_part(slot, 0, self.left)
            self.got_part(slot, 1, self.right)


def factor128(a):
    full = (8, 128)
    rows = lax.broadcasted_iota(jnp.int32, full, 0)
    lanes = lax.broadcasted_iota(jnp.int32, full, 1)
    strips = [a[8 * g : 8 * g + 8, :] for g in range(16)]
    units = [jnp.where(lanes == rows + 8 * g, 1.0, 0.0).astype(F32) for g in range(16)]
    uppers, inverses = [], []
    for g in range(16):
        s, t = strips[g], units[g]
        cols = [jnp.broadcast_to(s[:, 8 * g + m : 8 * g + m + 1], full) for m in range(8)]
        e = [[jnp.broadcast_to(cols[m][i : i + 1, :], full) for m in range(i + 1)] for i in range(8)]
        z = [jnp.broadcast_to(s[i : i + 1, :], full) for i in range(8)]
        y = [jnp.broadcast_to(t[i : i + 1, :], full) for i in range(8)]
        l = [[None] * 8 for _ in range(8)]
        r = []
        for k in range(8):
            r.append(pl.reciprocal(e[k][k], approx=True))
            for i in range(k + 1, 8):
                l[i][k] = e[i][k] * r[k]
            for j in range(k + 1, 8):
                for i in range(j, 8):
                    e[i][j] = e[i][j] - l[i][k] * e[j][k]
            for i in range(k + 1, 8):
                z[i] = z[i] - l[i][k] * z[k]
                y[i] = y[i] - l[i][k] * y[k]
        u = jnp.zeros(full, F32)
        w = jnp.zeros(full, F32)
        for i in range(8):
            q = lax.rsqrt(e[i][i])
            u = jnp.where(rows == i, z[i] * q, u)
            w = jnp.where(rows == i, y[i] * q, w)
        uppers.append(jnp.where(lanes >= rows + 8 * g, u, 0.0))
        inverses.append(w)
        top = g // 4 * 4 + 4
        if g + 1 < top:
            v, x = [None] * 8, [None] * 8
            for i in reversed(range(8)):
                v[i], x[i] = z[i] * r[i], y[i] * r[i]
                for m in range(i + 1, 8):
                    v[i] = v[i] - l[m][i] * v[m]
                    x[i] = x[i] - l[m][i] * x[m]
            for h in range(g + 1, top):
                c = [
                    jnp.broadcast_to(strips[h][:, 8 * g + m : 8 * g + m + 1], full)
                    for m in range(8)
                ]
                p = [c[m] * v[m] for m in range(8)]
                o = [c[m] * x[m] for m in range(8)]
                while len(p) > 1:
                    p = [p[2 * i] + p[2 * i + 1] for i in range(len(p) // 2)]
                    o = [o[2 * i] + o[2 * i + 1] for i in range(len(o) // 2)]
                strips[h] = strips[h] - p[0]
                units[h] = units[h] - o[0]
        elif top < 16:
            u = jnp.concatenate(uppers[top - 4 : top], 0)
            w = jnp.concatenate(inverses[top - 4 : top], 0)
            product = lax.dot_general(
                u,
                jnp.concatenate([u, w], 1),
                (((0,), (0,)), ((), ())),
                precision=HIGHEST,
                preferred_element_type=F32,
            )
            for h in range(top, 16):
                strips[h] = strips[h] - product[8 * h : 8 * h + 8, :128]
                units[h] = units[h] - product[8 * h : 8 * h + 8, 128:]
    return jnp.concatenate(uppers, 0), jnp.concatenate(inverses, 0)


def dot(a, b, dims=NN):
    return lax.dot_general(a, b, dims, precision=HIGHEST, preferred_element_type=jnp.float32)


def inverse_at(dinv, J):
    a, b, c, d = (dinv[J * 4 + i] for i in range(4))
    return jnp.concatenate([jnp.concatenate([a, b], 1), jnp.concatenate([c, d], 1)], 0)


def chol_loop(pv, dinv, between, nsteps=6):
    @pl.loop(0, nsteps)
    def _(J):
        ca = pl.multiple_of(J * 256, 256)
        cb = pl.multiple_of(J * 256 + 128, 128)
        for step, action in enumerate(between):
            pl.when(J == step)(action)
        ua, ia = factor128(pv[pl.ds(ca, 128), pl.ds(ca, 128)])
        la = ua.T
        pv[pl.ds(ca, 128), pl.ds(ca, 128)] = la
        wb = dot(pv[pl.ds(cb, 128), pl.ds(ca, 128)], ia, NT)
        pv[pl.ds(cb, 128), pl.ds(ca, 128)] = wb
        ub, ib = factor128(pv[pl.ds(cb, 128), pl.ds(cb, 128)] - dot(wb, wb, NT))
        pv[pl.ds(cb, 128), pl.ds(cb, 128)] = ub.T
        off = -dot(ib, dot(wb, ia))
        dinv[J * 4] = ia
        dinv[J * 4 + 1] = jnp.zeros((128, 128), F32)
        dinv[J * 4 + 2] = off
        dinv[J * 4 + 3] = ib
        inv = inverse_at(dinv, J)
        @pl.loop(J + 1, nsteps)
        def _(R):
            ro = pl.multiple_of(R * 256, 256)
            pv[pl.ds(ro, 256), pl.ds(ca, 256)] = dot(pv[pl.ds(ro, 256), pl.ds(ca, 256)], inv, NT)
        @pl.loop(J + 1, nsteps)
        def _(I):
            io = pl.multiple_of(I * 256, 256)
            wi = pv[pl.ds(io, 256), pl.ds(ca, 256)]
            @pl.loop(I, nsteps)
            def _(R):
                ro = pl.multiple_of(R * 256, 256)
                pv[pl.ds(ro, 256), pl.ds(io, 256)] -= dot(pv[pl.ds(ro, 256), pl.ds(ca, 256)], wi, NT)


def split(v):
    hi = v.astype(BF16)
    return hi, (v - hi.astype(F32)).astype(BF16)


def dot3(ah, al, bh, bl):
    a = jnp.concatenate([ah, ah, al], 1)
    b = jnp.concatenate([bh, bl, bh], 0)
    return lax.dot_general(a, b, NN, preferred_element_type=F32)


def solve_steps(g1, g2, l_ref, d_ref, xh, xl, yh, yl):
    for i in range(6):
        dh, dl = split(inverse_at(d_ref, i))
        lh, ll = split(l_ref[256 * i : 256 * i + 256, : 256 * i]) if i else (None, None)
        span = slice(256 * i, 256 * i + 256)
        blocks = slice(2 * i, 2 * i + 2)

        @pl.loop(0, 2)
        def _(n):
            cols = pl.ds(pl.multiple_of(n * 768, 256), 768)
            rhs = g1[blocks, :, cols].reshape(256, 768)
            if i:
                rhs = rhs - dot3(lh, ll, xh[: 256 * i, cols], xl[: 256 * i, cols])
            hi, lo = split(dot3(dh, dl, *split(rhs)))
            xh[span, cols] = hi
            xl[span, cols] = lo

        rhs = g2[blocks].reshape(256, 768)
        if i:
            rhs = rhs - dot3(lh, ll, *split(g2[: 2 * i].reshape(256 * i, 768)))
        g2[blocks] = dot3(dh, dl, *split(rhs)).reshape(2, 128, 768)
    for l in range(6):
        rows = slice(128 * l, 128 * l + 128)
        hi, lo = split(g2[:, :, rows].reshape(1536, 128).T)
        yh[rows, :] = hi
        yl[rows, :] = lo

    @pl.loop(0, 6)
    def _(t):
        rows = pl.ds(pl.multiple_of(t // 2 * 256, 256), 256)
        cols = pl.ds(pl.multiple_of(lax.rem(t, 2) * 768, 256), 768)
        l_ref[rows, cols] = dot3(yh[rows, :], yl[rows, :], xh[:, cols], xl[:, cols])


def place_steps(row, col, out_ref, yh, yl):
    @pl.when(row < 12)
    def _():
        out_ref[0:128, :] = jnp.zeros((128, 1536), F32)

    def place(block, m):
        lanes = pl.ds(pl.multiple_of(block * 128, 128), 128)
        values = yh[:, lanes].astype(F32) + yl[:, lanes].astype(F32)
        i = lax.broadcasted_iota(jnp.int32, values.shape, 0)
        j = lax.broadcasted_iota(jnp.int32, values.shape, 1)
        matrix_row = (i // 128 * 16 + row) * 128 + lax.rem(i, 128)
        out_ref[:, 128 * m : 128 * m + 128] = jnp.where(
            matrix_row >= block * 128 + j, values, 0.0
        )

    place(col, 0)

    @pl.when(col < 4)
    def _():
        place(col + 8, 1)


def panel_kernel(
    maps_ref,
    front_ref,
    child_ref,
    out_ref,
    arrived,
    g1,
    g2,
    pv,
    dinv,
    xh,
    xl,
    yh,
    yl,
    load_sem,
    block_send,
    first_sem,
    block_sem,
    early_sem,
    send_sem,
    head_sem,
    turn_sem,
    g1_sem,
    g2_sem,
    pv_sem,
):
    first = dinv.at[pl.ds(0, 16)]
    row, col = lax.axis_index("row"), lax.axis_index("col")
    h, x, k = row // 8, lax.rem(row, 8) // 2, lax.rem(row, 2)
    y, s = col // 2, lax.rem(col, 2)
    z = s * 2 + h
    me = row * 8 + col
    at_x = lambda p: h * 8 + lax.rem(p + 4, 4) * 2 + k
    at_y = lambda p: lax.rem(p + 4, 4) * 2 + s
    row_peers = [
        ((1 - h) * 8 + x * 2 + k, col),
        (at_x(x + 1), col),
        (at_x(x - 1), col),
        (h * 8 + x * 2 + 1 - k, col),
    ]
    col_peers = [(row, y * 2 + 1 - s), (row, at_y(y + 1)), (row, at_y(y - 1))]

    def block_at(i):
        return pl.ds(pl.multiple_of(i * 128, 128), 128)

    for i in range(8):
        for j in range(8):
            pltpu.make_async_copy(
                child_ref.at[pl.ds(128 * i, 128), pl.ds(128 * j, 128)],
                arrived.at[i * 8 + j],
                load_sem,
            ).start()
    pltpu.make_async_copy(arrived.at[pl.ds(0, 64)], arrived.at[pl.ds(64, 64)], load_sem).wait()
    run = lax.rem(row, 8)
    row_start = lax.rem(maps_ref[h, 8 * run], 8)
    col_start = lax.rem(maps_ref[h, 8 * col], 8)

    @pl.loop(0, 8)
    def _(r):
        i = lax.rem(r - row_start + 8, 8)

        @pl.loop(0, 8)
        def _(c):
            j = lax.rem(c - col_start + 8, 8)
            p = r * 8 + c
            out_ref[block_at(p // 12), block_at(lax.rem(p, 12))] = arrived[i * 8 + j]

    def packed(r, c):
        p = r * 8 + c
        return out_ref.at[block_at(p // 12), block_at(lax.rem(p, 12))]

    arrived[me] = packed(run, col)[...]

    def peer(o):
        o = lax.rem(o * 37, 128)
        to_x = lax.rem(x + lax.rem(o, 4), 4)
        to_y = lax.rem(y + lax.rem(o // 4, 4), 4)
        to_z = lax.rem(z + lax.rem(o // 16, 4), 4)
        to_k = lax.rem(k + o // 64, 2)
        return lax.rem(to_z, 2) * 8 + to_x * 2 + to_k, to_y * 2 + to_z // 2

    barrier = pltpu.get_barrier_semaphore()

    @pl.loop(1, 128)
    def _(o):
        pl.semaphore_signal(barrier, inc=1, device_id=peer(o), device_id_type=MESH)

    pl.semaphore_wait(barrier, 127)

    def is_first(to_row):
        return ((run == 0) & (to_row < 8)) | ((run == 1) & (to_row >= 8) & (to_row < 12))

    def send_first(base, count):
        @pl.loop(0, 8 * count)
        def _(t):
            i = lax.rem(t, count)
            to_row, to_col = base + i, lax.rem(col + t // count + i, 8)

            @pl.when((to_row != row) | (to_col != col))
            def _():
                pltpu.make_async_remote_copy(
                    src_ref=packed(lax.rem(to_row, 8), to_col),
                    dst_ref=first.at[h * 8 + col],
                    send_sem=block_send,
                    recv_sem=first_sem,
                    device_id=(to_row, to_col),
                    device_id_type=MESH,
                ).start()

            @pl.when((to_row == row) & (to_col == col))
            def _():
                first[h * 8 + col] = packed(lax.rem(to_row, 8), to_col)[...]

    pl.when(run == 0)(lambda: send_first(0, 8))
    pl.when(run == 1)(lambda: send_first(8, 4))

    def send_blocks(start, stop):
        @pl.loop(start, stop)
        def _(o):
            to_row, to_col = peer(o)

            @pl.when(jnp.logical_not(is_first(to_row)))
            def _():
                pltpu.make_async_remote_copy(
                    src_ref=packed(lax.rem(to_row, 8), to_col),
                    dst_ref=arrived.at[me],
                    send_sem=block_send,
                    recv_sem=block_sem.at[row],
                    device_id=(to_row, to_col),
                    device_id_type=MESH,
                ).start()

    def await_blocks(ref, sem, send=False):
        copy = pltpu.make_async_remote_copy(
            src_ref=ref,
            dst_ref=ref,
            send_sem=sem,
            recv_sem=sem,
            device_id=row_peers[0],
            device_id_type=MESH,
        )
        copy.wait_send() if send else copy.wait_recv()

    mine = jnp.where(row < 8, 0, 1)
    own_first = (row < 12) & (run == mine)

    @pl.when((row < 12) & own_first)
    def _():
        await_blocks(first.at[pl.ds(0, 15)], first_sem)

    @pl.when((row < 12) & jnp.logical_not(own_first))
    def _():
        await_blocks(first, first_sem)

    @pl.when((row >= 8) & (row < 12))
    def _():
        @pl.loop(0, 16)
        def _(i):
            arrived[(i // 8 * 8 + 1) * 8 + lax.rem(i, 8)] = first[i]

    early, mover = Mover(early_sem), Mover(send_sem)

    @pl.when(row < 12)
    def _():
        found = [run_of(maps_ref, member, row)[1] for member in range(2)]

        @pl.loop(0, 12)
        def _(m):
            total = front_ref[0:128, block_at(m)]
            for member in range(2):
                other, also = run_of(maps_ref, member, m * 8 + col)
                total = total + first[member * 8 + other] * (found[member] * also).astype(F32)
            g1[row, :, block_at(m)] = total

    def turned(m):
        return g1.at[row, :, pl.ds(128 * m, 128)]

    def head(e):
        return g2.at[e, :, pl.ds(0, 128)]

    own_head = (row < 12) & (run == col)
    for j in range(2):
        for o in range(8):
            target = (col + 8 * j, lax.rem(col + o, 8))
            early.send(
                lambda t=target: (row < 12) & ((t[0] != row) | (t[1] != col)),
                lambda j=j: turned(j),
                lambda: head_sem.at[row],
                target,
                lambda: head(row),
            )

    @pl.when(own_head)
    def _():
        g2[row, :, 0:128] = g1[row, :, block_at(h)]

    for j in range(2):
        target = (col + 8 * j, run)
        for l in range(1, 6):
            mover.send(
                lambda t=target: (row < 12) & ((t[0] != row) | (t[1] != col)),
                lambda j=j, l=l: turned(2 * l + j),
                lambda: turn_sem.at[row],
                target,
                lambda l=l: g2.at[row, :, pl.ds(128 * l, 128)],
            )

    @pl.when(own_head)
    def _():
        for l in range(1, 6):
            g2[row, :, 128 * l : 128 * l + 128] = g1[row, :, block_at(2 * l + h)]

    row_places = ((h, x, k), row_peers)
    wide = pl.ds(128, 1408)
    rows1 = RowGather(
        mover,
        lambda q: g1.at[q, :, wide],
        lambda q, i: g1.at[q, pl.ds(64 * i, 64), wide],
        g1_sem,
        lambda q: q < 12,
        row_places,
    )
    rest = pl.ds(128, 640)
    cols2 = ColGather(
        mover,
        lambda e: g2.at[e, :, rest],
        lambda e, i: g2.at[e, pl.ds(64 * i, 64), rest],
        g2_sem,
        ((y, s), col_peers),
    )
    pivots = [
        RowGather(
            early,
            lambda q, t=t: pv.at[pl.ds(512 * t, 512), block_at(q)],
            lambda q, i, t=t: pv.at[pl.ds(512 * t + 256 * i, 256), block_at(q)],
            pv_sem.at[t],
            lambda q, t=t: q < 4 * (t + 1),
            row_places,
        )
        for t in range(3)
    ]
    for e in range(12):
        await_copy(
            jnp.logical_not(own_head & (row == e)), head(e), head_sem.at[e], (e, lax.rem(row, 8))
        )

    @pl.when(row < 12)
    def _():
        @pl.loop(0, 12)
        def _(e):
            pv[block_at(e), block_at(row)] = g2[e, :, 0:128]

    for p in pivots:
        p.to_pair()
    for slot in (col, col + 8):
        await_copy(
            (slot < 12) & jnp.logical_not(own_head & (row == slot)),
            g2.at[lax.rem(slot, 12), :, rest],
            turn_sem.at[slot],
            (lax.rem(slot, 12), lax.rem(row, 8)),
        )
    cols2.to_pair()
    for p in pivots:
        p.to_ring()
    for p in pivots:
        p.forward()
    rows1.to_pair()
    cols2.to_ring()
    for p in pivots:
        p.to_mate()
    for p in pivots:
        p.finish()
    rows1.to_ring()
    early.finish()

    def step0():
        send_blocks(1, 16)

    def step1():
        cols2.forward()
        send_blocks(16, 36)

    def step2():
        rows1.forward()
        send_blocks(36, 64)

    def step3():
        send_blocks(64, 96)

    def step4():
        rows1.to_mate()
        send_blocks(96, 128)

    chol_loop(pv, dinv, [step0, step1, step2, step3, step4])
    cols2.finish()
    rows1.finish()
    mover.finish()
    solve_steps(g1, g2, pv, dinv, xh, xl, yh, yl)

    for q in range(16):
        early_row = (row < 12) & (lax.rem(jnp.int32(q), 8) == mine)
        wanted = jnp.logical_not(early_row)

        @pl.when(wanted & (row == q))
        def _():
            await_blocks(arrived.at[pl.ds(0, 7)], block_sem.at[q])

        @pl.when(wanted & (row != q))
        def _():
            await_blocks(arrived.at[pl.ds(0, 8)], block_sem.at[q])

    await_blocks(arrived.at[pl.ds(0, 127)], block_send, True)

    @pl.loop(0, 6)
    def _(l):
        runs = [run_of(maps_ref, member, l * 16 + row) for member in range(2)]

        @pl.loop(0, 12)
        def _(m):
            total = front_ref[block_at(l), block_at(m)] - pv[block_at(l), block_at(m)]
            for member in range(2):
                mine, found = runs[member]
                other, also = run_of(maps_ref, member, m * 8 + col)
                update = arrived[(member * 8 + mine) * 8 + other]
                total = total + update * (found * also).astype(F32)
            out_ref[block_at(l), block_at(m)] = total

    place_steps(row, col, out_ref, yh, yl)


def panel(maps, front, children):
    return pl.pallas_call(
        panel_kernel,
        out_shape=jax.ShapeDtypeStruct(front.shape, F32),
        in_specs=[SMEM, VMEM, pl.BlockSpec(memory_space=pl.ANY)],
        out_specs=VMEM,
        scratch_shapes=[
            pltpu.VMEM((128, 128, 128), F32),
            pltpu.VMEM((12, 128, 1536), F32),
            pltpu.VMEM((12, 128, 768), F32),
            pltpu.VMEM((1536, 1536), F32),
            pltpu.VMEM((24, 128, 128), F32),
            pltpu.VMEM((1536, 1536), BF16),
            pltpu.VMEM((1536, 1536), BF16),
            pltpu.VMEM((768, 1536), BF16),
            pltpu.VMEM((768, 1536), BF16),
            pltpu.SemaphoreType.DMA,
            pltpu.SemaphoreType.DMA,
            pltpu.SemaphoreType.DMA,
            pltpu.SemaphoreType.DMA((16,)),
            pltpu.SemaphoreType.DMA((96,)),
            pltpu.SemaphoreType.DMA((64,)),
            pltpu.SemaphoreType.DMA((16,)),
            pltpu.SemaphoreType.DMA((16,)),
            pltpu.SemaphoreType.DMA((2, 16)),
            pltpu.SemaphoreType.DMA((2, 16)),
            pltpu.SemaphoreType.DMA((3, 2, 16)),
        ],
        compiler_params=pltpu.CompilerParams(
            collective_id=0, has_side_effects=True, vmem_limit_bytes=63 * 2**20
        ),
        name="panel",
    )(maps, front, children)


def shards(front, children, maps):
    return panel(maps, front, children)


def solution(mesh):
    in_specs = (P("row", "col"), P("row", "col"), P())
    out_specs = P("row", "col")
    return jax.shard_map(shards, mesh=mesh, in_specs=in_specs, out_specs=out_specs, check_vma=False)
```

time: 365 us -> 342 us (0.937)
  the two profiles are of different devices: /device:TPU:39 before, /device:TPU:21 now
where the time goes in v3:
time: 342 us; the launch traced here: 341 us
  Pallas kernels  336 us (98%)
  local copies, waits for them, and re-layouts  4.84 us (1%)
    pallas_call x1, Pallas kernels, panel(): pl.pallas_call(panel_kernel, out_shape=jax.ShapeDtypeStruct(front.shape,...  336 us

profile of v3, /device:TPU:21, one launch (start us, length us, event | category | flops | bytes accessed | tf_op | source)
XLA Modules:
  0.0 341.3 jit_solution(6850998752341717822)
XLA Ops:
  0.0 336.5 %panel.1 = f32[768,1536]{1,0:T(8,128)} custom-call(s32[2,64]{1,0:T(2,128)} %maps_ref.1, f32[768,1536]{1,0:T(8,128)} %front_ref.1, f32[1024,1024]{1,0:T(8,128)} %child_ref.1), custom_call_target="tpu_custom_call" | custom-call | tf_op jit(solution)/shard_map/panel/pallas_call | solution.py:673
  336.5 4.8 %copy.5 = f32[768,1536]{1,0:T(8,128)} copy(f32[768,1536]{1,0:T(8,128)} %panel.1) | data formatting | bytes 9437184

commit v4 on v3

--- a/solution.py
+++ b/solution.py
@@ -455,10 +455,10 @@
     pl.when(run == 0)(lambda: send_first(0, 8))
     pl.when(run == 1)(lambda: send_first(8, 4))
 
-    def send_blocks(start, stop):
+    def send_blocks(start, stop, step):
         @pl.loop(start, stop)
-        def _(o):
-            to_row, to_col = peer(o)
+        def _(i):
+            to_row, to_col = peer(step(i))
 
             @pl.when(jnp.logical_not(is_first(to_row)))
             def _():
@@ -513,43 +513,52 @@
                 total = total + first[member * 8 + other] * (found[member] * also).astype(F32)
             g1[row, :, block_at(m)] = total
 
-    def turned(m):
-        return g1.at[row, :, pl.ds(128 * m, 128)]
-
-    def head(e):
-        return g2.at[e, :, pl.ds(0, 128)]
-
-    own_head = (row < 12) & (run == col)
+    def pivot_block(b):
+        return pv.at[block_at(row), block_at(b)]
+
     for j in range(2):
-        for o in range(8):
-            target = (col + 8 * j, lax.rem(col + o, 8))
+        block = col + 8 * j
+
+        @pl.when((row < 12) & (block <= row))
+        def _():
+            pv[block_at(row), block_at(block)] = g1[row, :, 128 * j : 128 * j + 128]
+
+        for o in range(1, 8):
             early.send(
-                lambda t=target: (row < 12) & ((t[0] != row) | (t[1] != col)),
-                lambda j=j: turned(j),
-                lambda: head_sem.at[row],
-                target,
-                lambda: head(row),
+                lambda b=block: (row < 12) & (b <= row),
+                lambda b=block: pivot_block(b),
+                lambda b=block: head_sem.at[b],
+                (row, lax.rem(col + o, 8)),
             )
 
-    @pl.when(own_head)
-    def _():
-        g2[row, :, 0:128] = g1[row, :, block_at(h)]
-
-    for j in range(2):
-        target = (col + 8 * j, run)
-        for l in range(1, 6):
-            mover.send(
-                lambda t=target: (row < 12) & ((t[0] != row) | (t[1] != col)),
-                lambda j=j, l=l: turned(2 * l + j),
-                lambda: turn_sem.at[row],
-                target,
-                lambda l=l: g2.at[row, :, pl.ds(128 * l, 128)],
+    own_turn = (row < 12) & (run == col)
+
+    def turn():
+        for j in range(2):
+            target = (col + 8 * j, run)
+            for l in range(6):
+                mover.send(
+                    lambda t=target: (row < 12) & ((t[0] != row) | (t[1] != col)),
+                    lambda j=j, l=l: g1.at[row, :, pl.ds(128 * (2 * l + j), 128)],
+                    lambda: turn_sem.at[row],
+                    target,
+                    lambda l=l: g2.at[row, :, pl.ds(128 * l, 128)],
+                )
+
+        @pl.when(own_turn)
+        def _():
+            for l in range(6):
+                g2[row, :, 128 * l : 128 * l + 128] = g1[row, :, block_at(2 * l + h)]
+
+    def turned():
+        for slot in (col, col + 8):
+            held = lax.rem(slot, 12)
+            await_copy(
+                (slot < 12) & jnp.logical_not(own_turn & (row == slot)),
+                g2.at[held],
+                turn_sem.at[slot],
+                (held, lax.rem(row, 8)),
             )
-
-    @pl.when(own_head)
-    def _():
-        for l in range(1, 6):
-            g2[row, :, 128 * l : 128 * l + 128] = g1[row, :, block_at(2 * l + h)]
 
     row_places = ((h, x, k), row_peers)
     wide = pl.ds(128, 1408)
@@ -561,52 +570,39 @@
         lambda q: q < 12,
         row_places,
     )
-    rest = pl.ds(128, 640)
     cols2 = ColGather(
         mover,
-        lambda e: g2.at[e, :, rest],
-        lambda e, i: g2.at[e, pl.ds(64 * i, 64), rest],
+        lambda e: g2.at[e],
+        lambda e, i: g2.at[e, pl.ds(64 * i, 64), :],
         g2_sem,
         ((y, s), col_peers),
     )
     pivots = [
         RowGather(
             early,
-            lambda q, t=t: pv.at[pl.ds(512 * t, 512), block_at(q)],
-            lambda q, i, t=t: pv.at[pl.ds(512 * t + 256 * i, 256), block_at(q)],
+            lambda q, t=t: pv.at[block_at(q), pl.ds(512 * t, 512)],
+            lambda q, i, t=t: pv.at[
+                pl.ds(pl.multiple_of(q * 128 + 64 * i, 64), 64), pl.ds(512 * t, 512)
+            ],
             pv_sem.at[t],
-            lambda q, t=t: q < 4 * (t + 1),
+            lambda q, t=t: (q < 12) & (q >= 4 * t),
             row_places,
         )
         for t in range(3)
     ]
-    for e in range(12):
+    for b in range(12):
         await_copy(
-            jnp.logical_not(own_head & (row == e)), head(e), head_sem.at[e], (e, lax.rem(row, 8))
+            (row < 12) & (b <= row) & (col != b % 8), pivot_block(b), head_sem.at[b], (row, b % 8)
         )
-
-    @pl.when(row < 12)
-    def _():
-        @pl.loop(0, 12)
-        def _(e):
-            pv[block_at(e), block_at(row)] = g2[e, :, 0:128]
-
     for p in pivots:
         p.to_pair()
-    for slot in (col, col + 8):
-        await_copy(
-            (slot < 12) & jnp.logical_not(own_head & (row == slot)),
-            g2.at[lax.rem(slot, 12), :, rest],
-            turn_sem.at[slot],
-            (lax.rem(slot, 12), lax.rem(row, 8)),
-        )
-    cols2.to_pair()
+    send_blocks(1, 32, lambda i: 4 * i)
     for p in pivots:
         p.to_ring()
     for p in pivots:
         p.forward()
+    turn()
     rows1.to_pair()
-    cols2.to_ring()
     for p in pivots:
         p.to_mate()
     for p in pivots:
@@ -614,23 +610,29 @@
     rows1.to_ring()
     early.finish()
 
+    def send_others(start, stop):
+        send_blocks(start, stop, lambda i: i // 3 * 4 + 1 + lax.rem(i, 3))
+
     def step0():
-        send_blocks(1, 16)
+        turned()
+        cols2.to_pair()
+        send_others(0, 8)
 
     def step1():
+        cols2.to_ring()
+        rows1.forward()
+        send_others(8, 24)
+
+    def step2():
         cols2.forward()
-        send_blocks(16, 36)
-
-    def step2():
-        rows1.forward()
-        send_blocks(36, 64)
+        rows1.to_mate()
+        send_others(24, 48)
 
     def step3():
-        send_blocks(64, 96)
+        send_others(48, 72)
 
     def step4():
-        rows1.to_mate()
-        send_blocks(96, 128)
+        send_others(72, 96)
 
     chol_loop(pv, dinv, [step0, step1, step2, step3, step4])
     cols2.finish()

time: 342 us -> 342 us (level)
  the two profiles are of different devices: /device:TPU:21 before, /device:TPU:84 now
where the time goes in v4:
time: 342 us; the launch traced here: 341 us
  Pallas kernels  337 us (99%)
  local copies, waits for them, and re-layouts  4.84 us (1%)
    pallas_call x1, Pallas kernels, panel(): pl.pallas_call(panel_kernel, out_shape=jax.ShapeDtypeStruct(front.shape,...  337 us

profile of v4, /device:TPU:84, one launch (start us, length us, event | category | flops | bytes accessed | tf_op | source)
XLA Modules:
  0.0 341.5 jit_solution(2936903754580751928)
XLA Ops:
  0.0 336.6 %panel.1 = f32[768,1536]{1,0:T(8,128)} custom-call(s32[2,64]{1,0:T(2,128)} %maps_ref.1, f32[768,1536]{1,0:T(8,128)} %front_ref.1, f32[1024,1024]{1,0:T(8,128)} %child_ref.1), custom_call_target="tpu_custom_call" | custom-call | tf_op jit(solution)/shard_map/panel/pallas_call | solution.py:675
  336.6 4.8 %copy.5 = f32[768,1536]{1,0:T(8,128)} copy(f32[768,1536]{1,0:T(8,128)} %panel.1) | data formatting | bytes 9437184

commit v5 on v4

--- a/solution.py
+++ b/solution.py
@@ -238,18 +238,22 @@
     return jnp.concatenate([jnp.concatenate([a, b], 1), jnp.concatenate([c, d], 1)], 0)
 
 
-def chol_loop(pv, dinv, between, nsteps=6):
+def chol_loop(pv, dinv, beside, nsteps=6):
     @pl.loop(0, nsteps)
     def _(J):
         ca = pl.multiple_of(J * 256, 256)
         cb = pl.multiple_of(J * 256 + 128, 128)
-        for step, action in enumerate(between):
-            pl.when(J == step)(action)
+        for step, action in beside.items():
+            if step % 2 == 0:
+                pl.when(J == step // 2)(action)
         ua, ia = factor128(pv[pl.ds(ca, 128), pl.ds(ca, 128)])
         la = ua.T
         pv[pl.ds(ca, 128), pl.ds(ca, 128)] = la
         wb = dot(pv[pl.ds(cb, 128), pl.ds(ca, 128)], ia, NT)
         pv[pl.ds(cb, 128), pl.ds(ca, 128)] = wb
+        for step, action in beside.items():
+            if step % 2 == 1:
+                pl.when(J == step // 2)(action)
         ub, ib = factor128(pv[pl.ds(cb, 128), pl.ds(cb, 128)] - dot(wb, wb, NT))
         pv[pl.ds(cb, 128), pl.ds(cb, 128)] = ub.T
         off = -dot(ib, dot(wb, ia))
@@ -283,33 +287,43 @@
     return lax.dot_general(a, b, NN, preferred_element_type=F32)
 
 
-def solve_steps(g1, g2, l_ref, d_ref, xh, xl, yh, yl):
+def solve_x(g1, l_ref, d_ref, xh, xl):
     for i in range(6):
         dh, dl = split(inverse_at(d_ref, i))
         lh, ll = split(l_ref[256 * i : 256 * i + 256, : 256 * i]) if i else (None, None)
-        span = slice(256 * i, 256 * i + 256)
-        blocks = slice(2 * i, 2 * i + 2)
 
         @pl.loop(0, 2)
         def _(n):
             cols = pl.ds(pl.multiple_of(n * 768, 256), 768)
-            rhs = g1[blocks, :, cols].reshape(256, 768)
+            rhs = g1[2 * i : 2 * i + 2, :, cols].reshape(256, 768)
             if i:
                 rhs = rhs - dot3(lh, ll, xh[: 256 * i, cols], xl[: 256 * i, cols])
             hi, lo = split(dot3(dh, dl, *split(rhs)))
-            xh[span, cols] = hi
-            xl[span, cols] = lo
-
-        rhs = g2[blocks].reshape(256, 768)
-        if i:
-            rhs = rhs - dot3(lh, ll, *split(g2[: 2 * i].reshape(256 * i, 768)))
-        g2[blocks] = dot3(dh, dl, *split(rhs)).reshape(2, 128, 768)
+            xh[256 * i : 256 * i + 256, cols] = hi
+            xl[256 * i : 256 * i + 256, cols] = lo
+
+
+def solve_y(g2, l_ref, d_ref, yh, yl):
+    for i in range(6):
+        dh, dl = split(inverse_at(d_ref, i))
+        lh, ll = split(l_ref[256 * i : 256 * i + 256, : 256 * i]) if i else (None, None)
+
+        @pl.loop(0, 3)
+        def _(n):
+            cols = pl.ds(pl.multiple_of(n * 256, 256), 256)
+            rhs = g2[2 * i : 2 * i + 2, :, cols].reshape(256, 256)
+            if i:
+                rhs = rhs - dot3(lh, ll, *split(g2[: 2 * i, :, cols].reshape(256 * i, 256)))
+            g2[2 * i : 2 * i + 2, :, cols] = dot3(dh, dl, *split(rhs)).reshape(2, 128, 256)
+
     for l in range(6):
         rows = slice(128 * l, 128 * l + 128)
         hi, lo = split(g2[:, :, rows].reshape(1536, 128).T)
         yh[rows, :] = hi
         yl[rows, :] = lo
 
+
+def update_steps(l_ref, xh, xl, yh, yl):
     @pl.loop(0, 6)
     def _(t):
         rows = pl.ds(pl.multiple_of(t // 2 * 256, 256), 256)
@@ -344,6 +358,7 @@
     front_ref,
     child_ref,
     out_ref,
+    mid,
     arrived,
     g1,
     g2,
@@ -354,6 +369,8 @@
     yh,
     yl,
     load_sem,
+    mid_send,
+    mid_sem,
     block_send,
     first_sem,
     block_sem,
@@ -370,7 +387,6 @@
     h, x, k = row // 8, lax.rem(row, 8) // 2, lax.rem(row, 2)
     y, s = col // 2, lax.rem(col, 2)
     z = s * 2 + h
-    me = row * 8 + col
     at_x = lambda p: h * 8 + lax.rem(p + 4, 4) * 2 + k
     at_y = lambda p: lax.rem(p + 4, 4) * 2 + s
     row_peers = [
@@ -391,7 +407,7 @@
                 arrived.at[i * 8 + j],
                 load_sem,
             ).start()
-    pltpu.make_async_copy(arrived.at[pl.ds(0, 64)], arrived.at[pl.ds(64, 64)], load_sem).wait()
+    pltpu.make_async_copy(arrived.at[pl.ds(0, 64)], mid, load_sem).wait()
     run = lax.rem(row, 8)
     row_start = lax.rem(maps_ref[h, 8 * run], 8)
     col_start = lax.rem(maps_ref[h, 8 * col], 8)
@@ -406,14 +422,13 @@
             p = r * 8 + c
             out_ref[block_at(p // 12), block_at(lax.rem(p, 12))] = arrived[i * 8 + j]
 
-    def packed(r, c):
-        p = r * 8 + c
+    def staged(p):
         return out_ref.at[block_at(p // 12), block_at(lax.rem(p, 12))]
 
-    arrived[me] = packed(run, col)[...]
+    for j in range(2):
+        mid[(run * 4 + y) * 2 + j] = staged(run * 8 + y * 2 + j)[...]
 
     def peer(o):
-        o = lax.rem(o * 37, 128)
         to_x = lax.rem(x + lax.rem(o, 4), 4)
         to_y = lax.rem(y + lax.rem(o // 4, 4), 4)
         to_z = lax.rem(z + lax.rem(o // 16, 4), 4)
@@ -428,48 +443,19 @@
 
     pl.semaphore_wait(barrier, 127)
 
-    def is_first(to_row):
-        return ((run == 0) & (to_row < 8)) | ((run == 1) & (to_row >= 8) & (to_row < 12))
-
-    def send_first(base, count):
-        @pl.loop(0, 8 * count)
-        def _(t):
-            i = lax.rem(t, count)
-            to_row, to_col = base + i, lax.rem(col + t // count + i, 8)
-
-            @pl.when((to_row != row) | (to_col != col))
-            def _():
-                pltpu.make_async_remote_copy(
-                    src_ref=packed(lax.rem(to_row, 8), to_col),
-                    dst_ref=first.at[h * 8 + col],
-                    send_sem=block_send,
-                    recv_sem=first_sem,
-                    device_id=(to_row, to_col),
-                    device_id_type=MESH,
-                ).start()
-
-            @pl.when((to_row == row) & (to_col == col))
-            def _():
-                first[h * 8 + col] = packed(lax.rem(to_row, 8), to_col)[...]
-
-    pl.when(run == 0)(lambda: send_first(0, 8))
-    pl.when(run == 1)(lambda: send_first(8, 4))
-
-    def send_blocks(start, stop, step):
-        @pl.loop(start, stop)
-        def _(i):
-            to_row, to_col = peer(step(i))
-
-            @pl.when(jnp.logical_not(is_first(to_row)))
-            def _():
-                pltpu.make_async_remote_copy(
-                    src_ref=packed(lax.rem(to_row, 8), to_col),
-                    dst_ref=arrived.at[me],
-                    send_sem=block_send,
-                    recv_sem=block_sem.at[row],
-                    device_id=(to_row, to_col),
-                    device_id_type=MESH,
-                ).start()
+    @pl.loop(1, 32)
+    def _(i):
+        o = lax.rem(i * 13, 32)
+        to_row, to_col = peer(lax.rem(o, 16) + o // 16 * 64)
+        for j in range(2):
+            pltpu.make_async_remote_copy(
+                src_ref=staged(lax.rem(to_row, 8) * 8 + to_col // 2 * 2 + j),
+                dst_ref=mid.at[(run * 4 + y) * 2 + j],
+                send_sem=mid_send,
+                recv_sem=mid_sem,
+                device_id=(to_row, to_col),
+                device_id_type=MESH,
+            ).start()
 
     def await_blocks(ref, sem, send=False):
         copy = pltpu.make_async_remote_copy(
@@ -482,36 +468,69 @@
         )
         copy.wait_send() if send else copy.wait_recv()
 
-    mine = jnp.where(row < 8, 0, 1)
-    own_first = (row < 12) & (run == mine)
-
-    @pl.when((row < 12) & own_first)
-    def _():
-        await_blocks(first.at[pl.ds(0, 15)], first_sem)
-
-    @pl.when((row < 12) & jnp.logical_not(own_first))
-    def _():
-        await_blocks(first, first_sem)
-
-    @pl.when((row >= 8) & (row < 12))
-    def _():
-        @pl.loop(0, 16)
-        def _(i):
-            arrived[(i // 8 * 8 + 1) * 8 + lax.rem(i, 8)] = first[i]
+    await_blocks(mid.at[pl.ds(0, 62)], mid_sem)
+    await_blocks(mid.at[pl.ds(0, 62)], mid_send, True)
+
+    def along_z(d):
+        to_z = lax.rem(z + d, 4)
+        return lax.rem(to_z, 2), to_z // 2
+
+    def stage(l, d):
+        to_h, to_s = along_z(d)
+        held, found = run_of(maps_ref, h, l * 16 + to_h * 8 + run)
+        for j in range(4):
+            block = mid[(held * 4 + j) * 2 + to_s] * found.astype(F32)
+            if d:
+                staged(((d - 1) * 6 + l) * 4 + j)[...] = block
+            elif isinstance(l, int):
+                first[z * 4 + j] = block
+            else:
+                arrived[(z * 5 + l - 1) * 4 + j] = block
+
+    def send_staged(l, d, dst, sem):
+        to_h, to_s = along_z(d)
+        for j in range(4):
+            pltpu.make_async_remote_copy(
+                src_ref=staged(((d - 1) * 6 + l) * 4 + j),
+                dst_ref=dst(j),
+                send_sem=block_send,
+                recv_sem=sem,
+                device_id=(to_h * 8 + run, y * 2 + to_s),
+                device_id_type=MESH,
+            ).start()
+
+    for d in (1, 3, 2):
+        stage(0, d)
+        send_staged(0, d, lambda j: first.at[z * 4 + j], first_sem)
+    stage(0, 0)
+
+    @pl.loop(1, 6)
+    def _(l):
+        for d in range(4):
+            stage(l, d)
+
+    def send_rest():
+        @pl.loop(1, 6)
+        def _(l):
+            for d in (1, 3, 2):
+                send_staged(l, d, lambda j: arrived.at[(z * 5 + l - 1) * 4 + j], block_sem)
+
+    await_blocks(first.at[pl.ds(0, 12)], first_sem)
 
     early, mover = Mover(early_sem), Mover(send_sem)
 
-    @pl.when(row < 12)
-    def _():
-        found = [run_of(maps_ref, member, row)[1] for member in range(2)]
-
-        @pl.loop(0, 12)
-        def _(m):
-            total = front_ref[0:128, block_at(m)]
-            for member in range(2):
-                other, also = run_of(maps_ref, member, m * 8 + col)
-                total = total + first[member * 8 + other] * (found[member] * also).astype(F32)
-            g1[row, :, block_at(m)] = total
+    own = jnp.minimum(row, 12)
+
+    def placed(blocks, count, m, total):
+        for member in range(2):
+            other, found = run_of(maps_ref, member, m * 8 + col)
+            update = blocks[(lax.rem(other, 2) * 2 + member) * count + other // 2]
+            total = total + update * found.astype(F32)
+        return total
+
+    @pl.loop(0, 12)
+    def _(m):
+        g1[own, :, block_at(m)] = placed(first, 4, m, front_ref[0:128, block_at(m)])
 
     def pivot_block(b):
         return pv.at[block_at(row), block_at(b)]
@@ -596,7 +615,6 @@
         )
     for p in pivots:
         p.to_pair()
-    send_blocks(1, 32, lambda i: 4 * i)
     for p in pivots:
         p.to_ring()
     for p in pivots:
@@ -607,65 +625,45 @@
         p.to_mate()
     for p in pivots:
         p.finish()
-    rows1.to_ring()
     early.finish()
 
-    def send_others(start, stop):
-        send_blocks(start, stop, lambda i: i // 3 * 4 + 1 + lax.rem(i, 3))
-
-    def step0():
+    def step2():
+        rows1.to_ring()
         turned()
         cols2.to_pair()
-        send_others(0, 8)
-
-    def step1():
-        cols2.to_ring()
-        rows1.forward()
-        send_others(8, 24)
-
-    def step2():
+
+    def step9():
         cols2.forward()
         rows1.to_mate()
-        send_others(24, 48)
-
-    def step3():
-        send_others(48, 72)
-
-    def step4():
-        send_others(72, 96)
-
-    chol_loop(pv, dinv, [step0, step1, step2, step3, step4])
+
+    chol_loop(
+        pv,
+        dinv,
+        {2: step2, 3: send_rest, 5: cols2.to_ring, 6: rows1.forward, 9: step9},
+    )
+    rows1.finish()
+    solve_x(g1, pv, dinv, xh, xl)
     cols2.finish()
-    rows1.finish()
     mover.finish()
-    solve_steps(g1, g2, pv, dinv, xh, xl, yh, yl)
-
-    for q in range(16):
-        early_row = (row < 12) & (lax.rem(jnp.int32(q), 8) == mine)
-        wanted = jnp.logical_not(early_row)
-
-        @pl.when(wanted & (row == q))
-        def _():
-            await_blocks(arrived.at[pl.ds(0, 7)], block_sem.at[q])
-
-        @pl.when(wanted & (row != q))
-        def _():
-            await_blocks(arrived.at[pl.ds(0, 8)], block_sem.at[q])
-
-    await_blocks(arrived.at[pl.ds(0, 127)], block_send, True)
-
-    @pl.loop(0, 6)
+    solve_y(g2, pv, dinv, yh, yl)
+    update_steps(pv, xh, xl, yh, yl)
+
+    await_blocks(arrived.at[pl.ds(0, 60)], block_sem)
+    await_blocks(arrived.at[pl.ds(0, 72)], block_send, True)
+
+    @pl.loop(0, 12)
+    def _(m):
+        out_ref[0:128, block_at(m)] = g1[own, :, block_at(m)] - pv[0:128, block_at(m)]
+
+    @pl.loop(1, 6)
     def _(l):
-        runs = [run_of(maps_ref, member, l * 16 + row) for member in range(2)]
-
         @pl.loop(0, 12)
         def _(m):
             total = front_ref[block_at(l), block_at(m)] - pv[block_at(l), block_at(m)]
             for member in range(2):
-                mine, found = runs[member]
-                other, also = run_of(maps_ref, member, m * 8 + col)
-                update = arrived[(member * 8 + mine) * 8 + other]
-                total = total + update * (found * also).astype(F32)
+                other, found = run_of(maps_ref, member, m * 8 + col)
+                held = (lax.rem(other, 2) * 2 + member) * 5 + l - 1
+                total = total + arrived[held * 4 + other // 2] * found.astype(F32)
             out_ref[block_at(l), block_at(m)] = total
 
     place_steps(row, col, out_ref, yh, yl)
@@ -678,8 +676,9 @@
         in_specs=[SMEM, VMEM, pl.BlockSpec(memory_space=pl.ANY)],
         out_specs=VMEM,
         scratch_shapes=[
-            pltpu.VMEM((128, 128, 128), F32),
-            pltpu.VMEM((12, 128, 1536), F32),
+            pltpu.VMEM((64, 128, 128), F32),
+            pltpu.VMEM((80, 128, 128), F32),
+            pltpu.VMEM((13, 128, 1536), F32),
             pltpu.VMEM((12, 128, 768), F32),
             pltpu.VMEM((1536, 1536), F32),
             pltpu.VMEM((24, 128, 128), F32),
@@ -690,7 +689,9 @@
             pltpu.SemaphoreType.DMA,
             pltpu.SemaphoreType.DMA,
             pltpu.SemaphoreType.DMA,
-            pltpu.SemaphoreType.DMA((16,)),
+            pltpu.SemaphoreType.DMA,
+            pltpu.SemaphoreType.DMA,
+            pltpu.SemaphoreType.DMA,
             pltpu.SemaphoreType.DMA((96,)),
             pltpu.SemaphoreType.DMA((64,)),
             pltpu.SemaphoreType.DMA((16,)),

time: 342 us -> 308 us (0.901)
  the two profiles are of different devices: /device:TPU:84 before, /device:TPU:39 now
where the time goes in v5:
time: 308 us; the launch traced here: 305 us
  Pallas kernels  300 us (97%)
  local copies, waits for them, and re-layouts  4.84 us (2%)
    pallas_call x1, Pallas kernels, panel(): pl.pallas_call(panel_kernel, out_shape=jax.ShapeDtypeStruct(front.shape,...  300 us

profile of v5, /device:TPU:39, one launch (start us, length us, event | category | flops | bytes accessed | tf_op | source)
XLA Modules:
  0.0 305.1 jit_solution(16199994432527120417)
XLA Ops:
  0.0 300.2 %panel.1 = f32[768,1536]{1,0:T(8,128)} custom-call(s32[2,64]{1,0:T(2,128)} %maps_ref.1, f32[768,1536]{1,0:T(8,128)} %front_ref.1, f32[1024,1024]{1,0:T(8,128)} %child_ref.1), custom_call_target="tpu_custom_call" | custom-call | tf_op jit(solution)/shard_map/panel/pallas_call | solution.py:673
  300.3 4.8 %copy.5 = f32[768,1536]{1,0:T(8,128)} copy(f32[768,1536]{1,0:T(8,128)} %panel.1) | data formatting | bytes 9437184

commit v6 on v5

--- a/solution.py
+++ b/solution.py
@@ -238,7 +238,21 @@
     return jnp.concatenate([jnp.concatenate([a, b], 1), jnp.concatenate([c, d], 1)], 0)
 
 
-def chol_loop(pv, dinv, beside, nsteps=6):
+def split(v):
+    hi = v.astype(BF16)
+    return hi, (v - hi.astype(F32)).astype(BF16)
+
+
+def pair(v, left):
+    hi, lo = split(v)
+    return jnp.concatenate([hi, hi, lo] if left else [hi, lo, hi], 1)
+
+
+def dot_pairs(a, b):
+    return lax.dot_general(a, b, NT, preferred_element_type=F32)
+
+
+def chol_loop(pv, dinv, beside, after_first, nsteps=6):
     @pl.loop(0, nsteps)
     def _(J):
         ca = pl.multiple_of(J * 256, 256)
@@ -257,28 +271,26 @@
         ub, ib = factor128(pv[pl.ds(cb, 128), pl.ds(cb, 128)] - dot(wb, wb, NT))
         pv[pl.ds(cb, 128), pl.ds(cb, 128)] = ub.T
         off = -dot(ib, dot(wb, ia))
+        pl.when(J == 0)(after_first)
         dinv[J * 4] = ia
         dinv[J * 4 + 1] = jnp.zeros((128, 128), F32)
         dinv[J * 4 + 2] = off
         dinv[J * 4 + 3] = ib
-        inv = inverse_at(dinv, J)
+        inv = pair(inverse_at(dinv, J), False)
         @pl.loop(J + 1, nsteps)
         def _(R):
             ro = pl.multiple_of(R * 256, 256)
-            pv[pl.ds(ro, 256), pl.ds(ca, 256)] = dot(pv[pl.ds(ro, 256), pl.ds(ca, 256)], inv, NT)
+            block = pair(pv[pl.ds(ro, 256), pl.ds(ca, 256)], True)
+            pv[pl.ds(ro, 256), pl.ds(ca, 256)] = dot_pairs(block, inv)
         @pl.loop(J + 1, nsteps)
         def _(I):
             io = pl.multiple_of(I * 256, 256)
-            wi = pv[pl.ds(io, 256), pl.ds(ca, 256)]
+            wi = pair(pv[pl.ds(io, 256), pl.ds(ca, 256)], False)
             @pl.loop(I, nsteps)
             def _(R):
                 ro = pl.multiple_of(R * 256, 256)
-                pv[pl.ds(ro, 256), pl.ds(io, 256)] -= dot(pv[pl.ds(ro, 256), pl.ds(ca, 256)], wi, NT)
-
-
-def split(v):
-    hi = v.astype(BF16)
-    return hi, (v - hi.astype(F32)).astype(BF16)
+                block = pair(pv[pl.ds(ro, 256), pl.ds(ca, 256)], True)
+                pv[pl.ds(ro, 256), pl.ds(io, 256)] -= dot_pairs(block, wi)
 
 
 def dot3(ah, al, bh, bl):
@@ -375,6 +387,7 @@
     first_sem,
     block_sem,
     early_sem,
+    later_sem,
     send_sem,
     head_sem,
     turn_sem,
@@ -400,6 +413,19 @@
     def block_at(i):
         return pl.ds(pl.multiple_of(i * 128, 128), 128)
 
+    def peer(o):
+        to_x = lax.rem(x + lax.rem(o, 4), 4)
+        to_y = lax.rem(y + lax.rem(o // 4, 4), 4)
+        to_z = lax.rem(z + lax.rem(o // 16, 4), 4)
+        to_k = lax.rem(k + o // 64, 2)
+        return lax.rem(to_z, 2) * 8 + to_x * 2 + to_k, to_y * 2 + to_z // 2
+
+    barrier = pltpu.get_barrier_semaphore()
+
+    @pl.loop(1, 128)
+    def _(o):
+        pl.semaphore_signal(barrier, inc=1, device_id=peer(o), device_id_type=MESH)
+
     for i in range(8):
         for j in range(8):
             pltpu.make_async_copy(
@@ -407,7 +433,8 @@
                 arrived.at[i * 8 + j],
                 load_sem,
             ).start()
-    pltpu.make_async_copy(arrived.at[pl.ds(0, 64)], mid, load_sem).wait()
+    loaded = arrived.at[pl.ds(0, 64)]
+    pltpu.make_async_copy(loaded, loaded, load_sem).wait()
     run = lax.rem(row, 8)
     row_start = lax.rem(maps_ref[h, 8 * run], 8)
     col_start = lax.rem(maps_ref[h, 8 * col], 8)
@@ -427,19 +454,6 @@
 
     for j in range(2):
         mid[(run * 4 + y) * 2 + j] = staged(run * 8 + y * 2 + j)[...]
-
-    def peer(o):
-        to_x = lax.rem(x + lax.rem(o, 4), 4)
-        to_y = lax.rem(y + lax.rem(o // 4, 4), 4)
-        to_z = lax.rem(z + lax.rem(o // 16, 4), 4)
-        to_k = lax.rem(k + o // 64, 2)
-        return lax.rem(to_z, 2) * 8 + to_x * 2 + to_k, to_y * 2 + to_z // 2
-
-    barrier = pltpu.get_barrier_semaphore()
-
-    @pl.loop(1, 128)
-    def _(o):
-        pl.semaphore_signal(barrier, inc=1, device_id=peer(o), device_id_type=MESH)
 
     pl.semaphore_wait(barrier, 127)
 
@@ -517,7 +531,7 @@
 
     await_blocks(first.at[pl.ds(0, 12)], first_sem)
 
-    early, mover = Mover(early_sem), Mover(send_sem)
+    early, later, mover = Mover(early_sem), Mover(later_sem), Mover(send_sem)
 
     own = jnp.minimum(row, 12)
 
@@ -598,7 +612,7 @@
     )
     pivots = [
         RowGather(
-            early,
+            later if t else early,
             lambda q, t=t: pv.at[block_at(q), pl.ds(512 * t, 512)],
             lambda q, i, t=t: pv.at[
                 pl.ds(pl.multiple_of(q * 128 + 64 * i, 64), 64), pl.ds(512 * t, 512)
@@ -617,15 +631,23 @@
         p.to_pair()
     for p in pivots:
         p.to_ring()
-    for p in pivots:
+    pivots[0].forward()
+    pivots[0].to_mate()
+    for p in pivots[1:]:
         p.forward()
     turn()
     rows1.to_pair()
-    for p in pivots:
-        p.to_mate()
-    for p in pivots:
-        p.finish()
+    pivots[0].finish()
     early.finish()
+
+    def step1():
+        for p in pivots[1:]:
+            p.to_mate()
+
+    def after_first():
+        for p in pivots[1:]:
+            p.finish()
+        later.finish()
 
     def step2():
         rows1.to_ring()
@@ -639,7 +661,8 @@
     chol_loop(
         pv,
         dinv,
-        {2: step2, 3: send_rest, 5: cols2.to_ring, 6: rows1.forward, 9: step9},
+        {1: step1, 2: step2, 3: send_rest, 5: cols2.to_ring, 6: rows1.forward, 9: step9},
+        after_first,
     )
     rows1.finish()
     solve_x(g1, pv, dinv, xh, xl)
@@ -692,7 +715,8 @@
             pltpu.SemaphoreType.DMA,
             pltpu.SemaphoreType.DMA,
             pltpu.SemaphoreType.DMA,
-            pltpu.SemaphoreType.DMA((96,)),
+            pltpu.SemaphoreType.DMA((48,)),
+            pltpu.SemaphoreType.DMA((48,)),
             pltpu.SemaphoreType.DMA((64,)),
             pltpu.SemaphoreType.DMA((16,)),
             pltpu.SemaphoreType.DMA((16,)),

time: 308 us -> 298 us (0.968)
  Pallas kernels: 300 us -> 292 us
    pallas_call x1, Pallas kernels: 300 us -> 292 us  [panel(): pl.pallas_call(panel_kernel, out_shape=jax.ShapeDtypeStruct(front.shape,...]
where the time goes in v6:
time: 298 us; the launch traced here: 297 us
  Pallas kernels  292 us (98%)
  local copies, waits for them, and re-layouts  4.84 us (2%)
    pallas_call x1, Pallas kernels, panel(): pl.pallas_call(panel_kernel, out_shape=jax.ShapeDtypeStruct(front.shape,...  292 us

profile of v6, /device:TPU:39, one launch (start us, length us, event | category | flops | bytes accessed | tf_op | source)
XLA Modules:
  0.0 296.9 jit_solution(1680989526449060939)
XLA Ops:
  0.0 292.0 %panel.1 = f32[768,1536]{1,0:T(8,128)} custom-call(s32[2,64]{1,0:T(2,128)} %maps_ref.1, f32[768,1536]{1,0:T(8,128)} %front_ref.1, f32[1024,1024]{1,0:T(8,128)} %child_ref.1), custom_call_target="tpu_custom_call" | custom-call | tf_op jit(solution)/shard_map/panel/pallas_call | solution.py:696
  292.0 4.8 %copy.5 = f32[768,1536]{1,0:T(8,128)} copy(f32[768,1536]{1,0:T(8,128)} %panel.1) | data formatting | bytes 9437184

commit v7 on v6

--- a/solution.py
+++ b/solution.py
@@ -635,8 +635,8 @@
     pivots[0].to_mate()
     for p in pivots[1:]:
         p.forward()
+    rows1.to_pair()
     turn()
-    rows1.to_pair()
     pivots[0].finish()
     early.finish()
 
@@ -649,19 +649,23 @@
             p.finish()
         later.finish()
 
-    def step2():
-        rows1.to_ring()
+    def step4():
         turned()
         cols2.to_pair()
-
-    def step9():
-        cols2.forward()
-        rows1.to_mate()
+        send_rest()
 
     chol_loop(
         pv,
         dinv,
-        {1: step1, 2: step2, 3: send_rest, 5: cols2.to_ring, 6: rows1.forward, 9: step9},
+        {
+            1: step1,
+            2: rows1.to_ring,
+            4: step4,
+            6: rows1.forward,
+            7: cols2.to_ring,
+            9: rows1.to_mate,
+            11: cols2.forward,
+        },
         after_first,
     )
     rows1.finish()

time: 298 us -> 299 us (level)
  no operation moved by 1% of the time
where the time goes in v7:
time: 299 us; the launch traced here: 298 us
  Pallas kernels  294 us (98%)
  local copies, waits for them, and re-layouts  4.84 us (2%)
    pallas_call x1, Pallas kernels, panel(): pl.pallas_call(panel_kernel, out_shape=jax.ShapeDtypeStruct(front.shape,...  294 us

profile of v7, /device:TPU:39, one launch (start us, length us, event | category | flops | bytes accessed | tf_op | source)
XLA Modules:
  0.0 298.4 jit_solution(234084820253769310)
XLA Ops:
  0.0 293.6 %panel.1 = f32[768,1536]{1,0:T(8,128)} custom-call(s32[2,64]{1,0:T(2,128)} %maps_ref.1, f32[768,1536]{1,0:T(8,128)} %front_ref.1, f32[1024,1024]{1,0:T(8,128)} %child_ref.1), custom_call_target="tpu_custom_call" | custom-call | tf_op jit(solution)/shard_map/panel/pallas_call | solution.py:700
  293.6 4.8 %copy.5 = f32[768,1536]{1,0:T(8,128)} copy(f32[768,1536]{1,0:T(8,128)} %panel.1) | data formatting | bytes 9437184

commit v8 on v6

--- a/solution.py
+++ b/solution.py
@@ -5,7 +5,6 @@
 from jax.experimental.pallas import tpu as pltpu
 from jax.sharding import PartitionSpec as P
 
-HIGHEST = lax.Precision.HIGHEST
 MESH = pl.DeviceIdType.MESH
 F32 = jnp.float32
 BF16 = jnp.bfloat16
@@ -216,21 +215,18 @@
         elif top < 16:
             u = jnp.concatenate(uppers[top - 4 : top], 0)
             w = jnp.concatenate(inverses[top - 4 : top], 0)
+            uh, ul = split(u)
+            bh, bl = split(jnp.concatenate([u, w], 1))
             product = lax.dot_general(
-                u,
-                jnp.concatenate([u, w], 1),
+                jnp.concatenate([uh, uh, ul], 0),
+                jnp.concatenate([bh, bl, bh], 0),
                 (((0,), (0,)), ((), ())),
-                precision=HIGHEST,
                 preferred_element_type=F32,
             )
             for h in range(top, 16):
                 strips[h] = strips[h] - product[8 * h : 8 * h + 8, :128]
                 units[h] = units[h] - product[8 * h : 8 * h + 8, 128:]
     return jnp.concatenate(uppers, 0), jnp.concatenate(inverses, 0)
-
-
-def dot(a, b, dims=NN):
-    return lax.dot_general(a, b, dims, precision=HIGHEST, preferred_element_type=jnp.float32)
 
 
 def inverse_at(dinv, J):
@@ -263,14 +259,14 @@
         ua, ia = factor128(pv[pl.ds(ca, 128), pl.ds(ca, 128)])
         la = ua.T
         pv[pl.ds(ca, 128), pl.ds(ca, 128)] = la
-        wb = dot(pv[pl.ds(cb, 128), pl.ds(ca, 128)], ia, NT)
+        wb = dot_pairs(pair(pv[pl.ds(cb, 128), pl.ds(ca, 128)], True), pair(ia, False))
         pv[pl.ds(cb, 128), pl.ds(ca, 128)] = wb
         for step, action in beside.items():
             if step % 2 == 1:
                 pl.when(J == step // 2)(action)
-        ub, ib = factor128(pv[pl.ds(cb, 128), pl.ds(cb, 128)] - dot(wb, wb, NT))
+        ub, ib = factor128(pv[pl.ds(cb, 128), pl.ds(cb, 128)] - dot_pairs(pair(wb, True), pair(wb, False)))
         pv[pl.ds(cb, 128), pl.ds(cb, 128)] = ub.T
-        off = -dot(ib, dot(wb, ia))
+        off = -dot3(*split(ib), *split(dot3(*split(wb), *split(ia))))
         pl.when(J == 0)(after_first)
         dinv[J * 4] = ia
         dinv[J * 4 + 1] = jnp.zeros((128, 128), F32)

time: 298 us -> 291 us (0.977)
  Pallas kernels: 292 us -> 284 us
    pallas_call x1, Pallas kernels: 292 us -> 284 us  [panel(): pl.pallas_call(panel_kernel, out_shape=jax.ShapeDtypeStruct(front.shape,...]
where the time goes in v8:
time: 291 us; the launch traced here: 289 us
  Pallas kernels  284 us (98%)
  local copies, waits for them, and re-layouts  4.84 us (2%)
    pallas_call x1, Pallas kernels, panel(): pl.pallas_call(panel_kernel, out_shape=jax.ShapeDtypeStruct(front.shape,...  284 us

profile of v8, /device:TPU:39, one launch (start us, length us, event | category | flops | bytes accessed | tf_op | source)
XLA Modules:
  0.0 289.0 jit_solution(9410277370342950142)
XLA Ops:
  0.0 284.2 %panel.1 = f32[768,1536]{1,0:T(8,128)} custom-call(s32[2,64]{1,0:T(2,128)} %maps_ref.1, f32[768,1536]{1,0:T(8,128)} %front_ref.1, f32[1024,1024]{1,0:T(8,128)} %child_ref.1), custom_call_target="tpu_custom_call" | custom-call | tf_op jit(solution)/shard_map/panel/pallas_call | solution.py:692
  284.2 4.8 %copy.5 = f32[768,1536]{1,0:T(8,128)} copy(f32[768,1536]{1,0:T(8,128)} %panel.1) | data formatting | bytes 9437184
